TPU v7x, 256 devices: a whole 4x4x8 slice. The times are simulated.
256 devices in a mesh: gx: 8 (over z), gy: 4 (over y_lo, core), gz: 8 (over x, y_hi).
Axes of the slice: x: 4, y: 4 (y_hi: 2, y_lo: 2; y = y_hi * 2 + y_lo), z: 8, core: 2. Of those that a mesh axis runs over, the one named last changes fastest.
Arguments:
- features: bfloat16 [64, 16, 32, 1024], P(None, 'gx', 'gy', 'gz'), may hold values from -6 to 6
- dest_bricks: int32 [8192, 1], P(('gx', 'gy', 'gz')), may hold values from 0 to 31
- cell_ids: int32 [8192, 64], P(('gx', 'gy', 'gz')), may hold values from 0 to 2047
- cic_masses: bfloat16 [8192, 64], P(('gx', 'gy', 'gz')), may hold values from 0.25 to 4
- live_counts: int32 [256], P(('gx', 'gy', 'gz')), may hold values from 8 to 32
- style_vector: float32 [512], replicated, may hold values from -6 to 6
- affine_first: float32 [512, 64], replicated, may hold values from -0.25 to 0.25
- kernel_first: bfloat16 [27, 64, 64], replicated, may hold values from -0.15625 to 0.15625
- bias_first: float32 [64], replicated, may hold values from -0.5 to 0.5
- gain_first: float32 [64], replicated, may hold values from 1 to 4
- affine_second: float32 [512, 64], replicated, may hold values from -0.25 to 0.25
- kernel_second: bfloat16 [27, 64, 64], replicated, may hold values from -0.15625 to 0.15625
- bias_second: float32 [64], replicated, may hold values from -0.5 to 0.5
- gain_second: float32 [64], replicated, may hold values from 1 to 4
Outputs:
- upsampled: bfloat16 [64, 16, 32, 1024], P(None, 'gx', 'gy', 'gz')
All inputs are finite; a program needn't handle non-finite values.
Results may differ from a plain program's by a relative error of at most 0.0054.
Values may be sent and summed in bfloat16 or wider, within the bound.
A program may use at most 64 MiB of HBM per device.

v0:
```python
import jax
import jax.numpy as jnp
from jax import lax
from jax.sharding import PartitionSpec as P


def extended(cells, sides, width):
    for axis, dim in sides:
        count = lax.axis_size(axis)
        head = lax.slice_in_dim(cells, 0, width, axis=dim)
        tail = lax.slice_in_dim(cells, cells.shape[dim] - width, cells.shape[dim], axis=dim)
        cells = jnp.concatenate(
            [
                lax.ppermute(tail, axis, [(i, (i + 1) % count) for i in range(count)]),
                cells,
                lax.ppermute(head, axis, [((i + 1) % count, i) for i in range(count)]),
            ],
            axis=dim,
        )
    return cells


def modulate(kernel, style_vector, affine):
    styles = (
        jnp.dot(
            style_vector[None, :],
            affine,
            precision=lax.Precision.HIGHEST,
            preferred_element_type=jnp.float32,
        )[0]
        + 1.0
    )
    scaled = kernel.astype(jnp.float32) * styles[None, None, :]
    demod = lax.rsqrt(jnp.sum(scaled * scaled, axis=(0, 2)) + 1e-08)
    return (scaled * demod[None, :, None]).astype(jnp.bfloat16)


def activate(values):
    return jnp.where(values >= 0, values, 0.2 * values) * jnp.sqrt(jnp.float32(2.0))


def convolve(padded, modulated):
    chans = padded.shape[0]
    out_x = padded.shape[1] - 2
    out_y = padded.shape[2] - 2
    out_z = padded.shape[3] - 2
    outputs = modulated.shape[1]
    summed = jnp.zeros((outputs, out_x * out_y * out_z), jnp.float32)
    for offset_x in range(3):
        for offset_y in range(3):
            stacked = jnp.concatenate(
                [
                    padded[
                        :,
                        offset_x : offset_x + out_x,
                        offset_y : offset_y + out_y,
                        offset_z : offset_z + out_z,
                    ]
                    for offset_z in range(3)
                ],
                axis=0,
            ).reshape(3 * chans, -1)
            first_offset = offset_x * 9 + offset_y * 3
            matrix = (
                modulated[first_offset : first_offset + 3]
                .transpose(1, 0, 2)
                .reshape(outputs, 3 * chans)
            )
            summed = summed + jnp.dot(matrix, stacked, preferred_element_type=jnp.float32)
    return summed.reshape(outputs, out_x, out_y, out_z)


def finish_layer(convolved, bias, gain, density):
    return activate(
        convolved + gain[:, None, None, None] * density[None] + bias[:, None, None, None]
    )


def shards(
    features,
    dest_bricks,
    cell_ids,
    cic_masses,
    live_counts,
    style_vector,
    affine_first,
    kernel_first,
    bias_first,
    gain_first,
    affine_second,
    kernel_second,
    bias_second,
    gain_second,
):
    size_x = features.shape[1]
    size_y = features.shape[2]
    size_z = features.shape[3]
    cell_total = size_x * size_y * size_z
    slab_size = lax.axis_size("gy") * lax.axis_size("gz")
    per_block = cell_ids.shape[1]
    cell_iota = jnp.arange(cell_total, dtype=jnp.int32)
    live_count = live_counts[0]
    brick_iota = jnp.arange(slab_size, dtype=jnp.int32)

    def paint_step(position, partial_value):
        first_block = position * 4
        block_dest = lax.dynamic_slice_in_dim(dest_bricks, first_block, 4, 0)[:, 0]
        block_cells = lax.dynamic_slice_in_dim(cell_ids, first_block, 4, 0)
        block_mass = lax.dynamic_slice_in_dim(cic_masses, first_block, 4, 0)
        live_mask = first_block + jnp.arange(4, dtype=jnp.int32) < live_count
        block_mass = block_mass * live_mask[:, None].astype(jnp.bfloat16)
        dest_onehot = (block_dest[:, None] == brick_iota[None, :]).astype(jnp.bfloat16)
        spread = (dest_onehot[:, None, :] * block_mass[:, :, None]).reshape(
            4 * per_block, slab_size
        )
        cell_onehot = (block_cells.reshape(-1)[:, None] == cell_iota[None, :]).astype(jnp.bfloat16)
        return partial_value + jnp.dot(spread.T, cell_onehot, preferred_element_type=jnp.float32)

    painted = lax.fori_loop(
        0, (live_count + 3) // 4, paint_step, jnp.zeros((slab_size, cell_total), jnp.float32)
    )
    own_density = lax.psum_scatter(painted, ("gy", "gz"), scatter_dimension=0, tiled=True)
    density = own_density.reshape(size_x, size_y, size_z)
    modulated_first = modulate(kernel_first, style_vector, affine_first)
    modulated_second = modulate(kernel_second, style_vector, affine_second)
    padded = extended(features, (("gx", 1), ("gy", 2), ("gz", 3)), 1)
    hidden = finish_layer(
        convolve(padded, modulated_first), bias_first, gain_first, density
    ).astype(jnp.bfloat16)
    hidden_padded = extended(hidden, (("gx", 1), ("gy", 2), ("gz", 3)), 1)
    result = finish_layer(
        convolve(hidden_padded, modulated_second), bias_second, gain_second, density
    )
    return result.astype(jnp.bfloat16)


def solution(mesh):
    return jax.shard_map(
        shards,
        mesh=mesh,
        in_specs=(
            P(None, "gx", "gy", "gz"),
            P(("gx", "gy", "gz"), None),
            P(("gx", "gy", "gz"), None),
            P(("gx", "gy", "gz"), None),
            P(("gx", "gy", "gz")),
            P(),
            P(),
            P(),
            P(),
            P(),
            P(),
            P(),
            P(),
            P(),
        ),
        out_specs=P(None, "gx", "gy", "gz"),
        check_vma=False,
    )
```

profile of v0, /device:TPU:1, one launch (start us, length us, event | category | flops | bytes accessed | tf_op | source)
XLA Modules:
  0.0 224.4 jit_solution(7311847732096407512)
XLA Ops:
  6.5 1.1 copy.109
  7.6 2.5 %collective-permute-start = (bf16[64,1,8,128]{3,0,2,1:T(8,128)(2,1)S(1)}, bf16[64,1,8,128]{3,0,2,1:T(8,128)(2,1)S(1)}, u32[]{:S(2)}, u32[]{:S(2)}) collective-permute-start(bf16[64,1,8,128]{3,0,2,1:T(8,128)(2,1)S(1)} %get-tuple-element.177), channel_id=1, source_target_pairs={{0,32},{32,64},{64,96},{96,128},{128,160},{160,192},{192,224},{224... | collective-permute-start | bytes 393224 | tf_op jit(solution)/shard_map/ppermute | solution.py:14
  10.2 4.0 %collective-permute-start.1 = (bf16[64,1,8,128]{3,0,2,1:T(8,128)(2,1)S(1)}, bf16[64,1,8,128]{3,0,2,1:T(8,128)(2,1)S(1)}, u32[]{:S(2)}, u32[]{:S(2)}) collective-permute-start(bf16[64,1,8,128]{3,0,2,1:T(8,128)(2,1)S(1)} %get-tuple-element.176), channel_id=1, source_target_pairs={{32,0},{64,32},{96,64},{128,96},{160,128},{192,160},{224,192},{0,2... | collective-permute-start | bytes 393224 | tf_op jit(solution)/shard_map/ppermute | solution.py:16
  14.9 15.6 %while.11 = (s32[]{:T(128)}, f32[32,2048]{1,0:T(8,128)S(1)}, s32[]{:T(128)}, s32[32,1]{0,1:T(1,128)S(1)}, bf16[32,64]{1,0:T(8,128)(2,1)}, /*index=5*/s32[]{:T(12...) while((s32[]{:T(128)}, f32[32,2048]{1,0:T(8,128)S(1)}, ...), condition=%wide.region_3.4_spmd.clone, body=%wide.region_2.3_spmd.clone.sunk | while | flops 34153744 | bytes 565487 | solution.py:119
  15.0 0.7 compare_convert_fusion.2
  15.7 0.8 dynamic-slice_multiply_fusion.2
  18.8 0.8 dynamic-slice_multiply_fusion.2
  21.9 0.8 dynamic-slice_multiply_fusion.2
  25.0 0.8 dynamic-slice_multiply_fusion.2
  28.2 0.8 dynamic-slice_multiply_fusion.2
  32.1 0.7 copy.108
  32.8 0.7 copy.117
  33.5 0.7 copy.120
  34.2 0.7 copy.122
  34.9 0.7 copy.124
  35.7 0.7 copy.127
  36.4 0.7 copy.129
  39.1 2.2 collective-permute-start.2
  41.3 8.3 %collective-permute-start.3 = (bf16[64,4,1,128]{3,0,2,1:T(8,128)(2,1)S(1)}, bf16[64,4,1,128]{3,0,2,1:T(8,128)(2,1)S(1)}, u32[]{:S(2)}, u32[]{:S(2)}) collective-permute-start(bf16[64,4,1,128]{3,0,2,1:T(8,128)(2,1)S(1)} %get-tuple-element.149), channel_id=1, source_target_pairs={{8,0},{16,8},{24,16},{0,24},{9,1},{17,9},{25,17},{1,25},{10,2},{18... | collective-permute-start | bytes 196616 | tf_op jit(solution)/shard_map/ppermute | solution.py:16
  49.6 102.7 %all-reduce.3.cloned.1.call-done = f32[32,2048]{1,0:T(8,128)} async-done(((f32[32,2048]{1,0:T(8,128)}), f32[32,2048]{1,0:T(8,128)}) %all-reduce.3.cloned.1.call-update) | async-done | bytes 262160
  152.3 2.0 constant_dynamic-slice_fusion.2
  154.7 1.1 copy.160
  155.8 2.2 collective-permute-start.4
  158.4 3.1 %collective-permute-start.5 = (bf16[64,4,10,1]{0,2,3,1:T(8,128)(2,1)S(1)}, bf16[64,4,10,1]{0,2,3,1:T(8,128)(2,1)}, u32[]{:S(2)}, u32[]{:S(2)}) collective-permute-start(bf16[64,4,10,1]{0,2,3,1:T(8,128)(2,1)S(1)} %copy.161), channel_id=1, source_target_pairs={{1,0},{2,1},{3,2},{4,3},{5,4},{6,5},{7,6},{0,7},{9,8},{10,9},{11,1... | collective-permute-start | bytes 15368 | tf_op jit(solution)/shard_map/ppermute | solution.py:16
  161.5 0.8 fusion.67
  163.0 1.1 copy.115
  164.1 0.9 maximum_maximum_fusion
  165.1 1.1 fusion.73
  177.1 1.3 collective-permute-start.6
  178.4 1.8 collective-permute-start.7
  180.4 2.1 collective-permute-done.6
  182.6 4.0 %collective-permute-start.8 = (bf16[64,4,1,128]{3,0,2,1:T(8,128)(2,1)S(1)}, bf16[64,4,1,128]{3,0,2,1:T(8,128)(2,1)S(1)}, u32[]{:S(2)}, u32[]{:S(2)}) collective-permute-start(bf16[64,4,1,128]{3,0,2,1:T(8,128)(2,1)S(1)} %get-tuple-element.142), channel_id=1, source_target_pairs={{0,8},{8,16},{16,24},{24,0},{1,9},{9,17},{17,25},{25,1},{2,10},{10... | collective-permute-start | bytes 196616 | tf_op jit(solution)/shard_map/ppermute | solution.py:14
  186.6 0.7 copy.107
  187.3 0.7 copy.142
  188.0 0.7 copy.144
  188.8 0.7 copy.146
  189.5 0.7 copy.148
  190.2 0.7 copy.150
  190.9 0.7 copy.152
  191.6 0.7 copy.154
  192.3 0.7 copy.156
  194.1 1.1 copy.162
  195.1 2.0 collective-permute-start.10
  197.6 3.5 %collective-permute-start.11 = (bf16[64,4,10,1]{0,2,3,1:T(8,128)(2,1)S(1)}, bf16[64,4,10,1]{0,2,3,1:T(8,128)(2,1)}, u32[]{:S(2)}, u32[]{:S(2)}) collective-permute-start(bf16[64,4,10,1]{0,2,3,1:T(8,128)(2,1)S(1)} %copy.163), channel_id=1, source_target_pairs={{1,0},{2,1},{3,2},{4,3},{5,4},{6,5},{7,6},{0,7},{9,8},{10,9},{11,1... | collective-permute-start | bytes 15368 | tf_op jit(solution)/shard_map/ppermute | solution.py:16
  202.3 1.1 copy.140
  203.4 1.6 maximum_maximum_fusion.1
  205.5 0.7 fusion.72
  216.7 0.9 copy.159
  (221 shorter events, 40.1 us)
Async XLA Ops:
  6.5 24.8 %copy-start = (f32[512,64]{0,1:T(8,128)S(1)}, f32[512,64]{0,1:T(8,128)}, u32[]{:S(2)}) copy-start(f32[512,64]{0,1:T(8,128)} %param.22) | copy-start | bytes 393220
  6.5 8.4 %copy-start.39 = (s32[32,1]{0,1:T(1,128)S(1)}, s32[32,1]{0,1:T(1,128)}, u32[]{:S(2)}) copy-start(s32[32,1]{0,1:T(1,128)} %param.17) | copy-start | bytes 388
  6.5 145.7 %all-reduce.3.cloned.1.call-start = ((), (), s32[]{:S(2)}) async-start(), calls=%async_computation | async-start | bytes 524288
  7.6 31.3 %collective-permute-start = (bf16[64,1,8,128]{3,0,2,1:T(8,128)(2,1)S(1)}, bf16[64,1,8,128]{3,0,2,1:T(8,128)(2,1)S(1)}, u32[]{:S(2)}, u32[]{:S(2)}) collective-permute-start(bf16[64,1,8,128]{3,0,2,1:T(8,128)(2,1)S(1)} %get-tuple-element.177), channel_id=1, source_target_pairs={{0,32},{32,64},{64,96},{96,128},{128,160},{160,192},{192,224},{224... | collective-permute-start | bytes 393224 | tf_op jit(solution)/shard_map/ppermute | solution.py:14
  10.2 28.9 %collective-permute-start.1 = (bf16[64,1,8,128]{3,0,2,1:T(8,128)(2,1)S(1)}, bf16[64,1,8,128]{3,0,2,1:T(8,128)(2,1)S(1)}, u32[]{:S(2)}, u32[]{:S(2)}) collective-permute-start(bf16[64,1,8,128]{3,0,2,1:T(8,128)(2,1)S(1)} %get-tuple-element.176), channel_id=1, source_target_pairs={{32,0},{64,32},{96,64},{128,96},{160,128},{192,160},{224,192},{0,2... | collective-permute-start | bytes 393224 | tf_op jit(solution)/shard_map/ppermute | solution.py:16
  14.9 16.4 %copy-start.31 = (f32[512]{0:T(512)S(1)}, f32[512]{0:T(512)}, u32[]{:S(2)}) copy-start(f32[512]{0:T(512)} %param.21) | copy-start | bytes 6148
  14.9 16.6 %copy-start.3 = (bf16[27,64,64]{2,1,0:T(8,128)(2,1)S(1)}, bf16[27,64,64]{2,1,0:T(8,128)(2,1)}, u32[]{:S(2)}) copy-start(bf16[27,64,64]{2,1,0:T(8,128)(2,1)} %param.23) | copy-start | bytes 663556
  30.6 0.7 copy-start.2
  31.8 5.4 %copy-start.29 = (f32[512,64]{0,1:T(8,128)S(1)}, f32[512,64]{0,1:T(8,128)}, u32[]{:S(2)}) copy-start(f32[512,64]{0,1:T(8,128)} %param.26) | copy-start | bytes 393220
  31.9 5.7 %copy-start.40 = (u32[256]{0:T(256)S(1)}, u32[256]{0:T(256)}, u32[]{:S(2)}) copy-start(u32[256]{0:T(256)} %constant.45) | copy-start | bytes 3076
  31.9 6.2 %copy-start.4 = (bf16[27,64,64]{2,1,0:T(8,128)(2,1)S(1)}, bf16[27,64,64]{2,1,0:T(8,128)(2,1)}, u32[]{:S(2)}) copy-start(bf16[27,64,64]{2,1,0:T(8,128)(2,1)} %param.27) | copy-start | bytes 663556
  32.1 6.9 %copy-start.5 = (bf16[64,2,8,128]{3,2,1,0:T(8,128)(2,1)S(1)}, bf16[64,2,8,128]{3,2,1,0:T(8,128)(2,1)}, u32[]{:S(2)}) copy-start(bf16[64,2,8,128]{3,2,1,0:T(8,128)(2,1)} %param.16) | copy-start | bytes 786436
  37.5 116.8 %copy-start.32 = (f32[64]{0:T(128)}, f32[64]{0:T(128)S(1)}, u32[]{:S(2)}) copy-start(f32[64]{0:T(128)S(1)} %fusion.9) | copy-start | bytes 772
  38.9 115.3 %copy-start.9 = (bf16[64,1,8,128]{3,0,2,1:T(8,128)(2,1)}, bf16[64,1,8,128]{3,0,2,1:T(8,128)(2,1)S(1)}, u32[]{:S(2)}) copy-start(bf16[64,1,8,128]{3,0,2,1:T(8,128)(2,1)S(1)} %collective-permute-done) | copy-start | bytes 393220
  39.1 115.2 %copy-start.11 = (bf16[64,1,8,128]{3,0,2,1:T(8,128)(2,1)}, bf16[64,1,8,128]{3,0,2,1:T(8,128)(2,1)S(1)}, u32[]{:S(2)}) copy-start(bf16[64,1,8,128]{3,0,2,1:T(8,128)(2,1)S(1)} %collective-permute-done.1) | copy-start | bytes 393220
  39.1 115.1 %collective-permute-start.2 = (bf16[64,4,1,128]{3,0,2,1:T(8,128)(2,1)S(1)}, bf16[64,4,1,128]{3,0,2,1:T(8,128)(2,1)S(1)}, u32[]{:S(2)}, u32[]{:S(2)}) collective-permute-start(bf16[64,4,1,128]{3,0,2,1:T(8,128)(2,1)S(1)} %get-tuple-element.148), channel_id=1, source_target_pairs={{0,8},{8,16},{16,24},{24,0},{1,9},{9,17},{17,25},{25,1},{2,10},{10... | collective-permute-start | bytes 196616 | tf_op jit(solution)/shard_map/ppermute | solution.py:14
  41.3 112.9 %collective-permute-start.3 = (bf16[64,4,1,128]{3,0,2,1:T(8,128)(2,1)S(1)}, bf16[64,4,1,128]{3,0,2,1:T(8,128)(2,1)S(1)}, u32[]{:S(2)}, u32[]{:S(2)}) collective-permute-start(bf16[64,4,1,128]{3,0,2,1:T(8,128)(2,1)S(1)} %get-tuple-element.149), channel_id=1, source_target_pairs={{8,0},{16,8},{24,16},{0,24},{9,1},{17,9},{25,17},{1,25},{10,2},{18... | collective-permute-start | bytes 196616 | tf_op jit(solution)/shard_map/ppermute | solution.py:16
  155.8 6.5 %collective-permute-start.4 = (bf16[64,4,10,1]{0,2,3,1:T(8,128)(2,1)}, bf16[64,4,10,1]{0,2,3,1:T(8,128)(2,1)S(1)}, u32[]{:S(2)}, u32[]{:S(2)}) collective-permute-start(bf16[64,4,10,1]{0,2,3,1:T(8,128)(2,1)} %copy.160), channel_id=1, source_target_pairs={{0,1},{1,2},{2,3},{3,4},{4,5},{5,6},{6,7},{7,0},{8,9},{9,10},{10,1... | collective-permute-start | bytes 15368 | tf_op jit(solution)/shard_map/ppermute | solution.py:14
  158.4 4.6 %collective-permute-start.5 = (bf16[64,4,10,1]{0,2,3,1:T(8,128)(2,1)S(1)}, bf16[64,4,10,1]{0,2,3,1:T(8,128)(2,1)}, u32[]{:S(2)}, u32[]{:S(2)}) collective-permute-start(bf16[64,4,10,1]{0,2,3,1:T(8,128)(2,1)S(1)} %copy.161), channel_id=1, source_target_pairs={{1,0},{2,1},{3,2},{4,3},{5,4},{6,5},{7,6},{0,7},{9,8},{10,9},{11,1... | collective-permute-start | bytes 15368 | tf_op jit(solution)/shard_map/ppermute | solution.py:16
  166.3 1.0 copy-start.6
  168.5 0.9 copy-start.10
  168.5 1.0 copy-start.12
  171.4 1.1 copy-start.19
  171.9 0.8 copy-start.18
  172.4 0.8 copy-start.17
  173.1 0.8 copy-start.16
  173.5 0.8 copy-start.15
  174.2 0.8 copy-start.14
  174.6 0.8 copy-start.13
  176.4 3.9 %copy-start.33 = (f32[64]{0:T(128)S(1)}, f32[64]{0:T(128)}, u32[]{:S(2)}) copy-start(f32[64]{0:T(128)} %copy-done.32) | copy-start | bytes 772
  176.4 3.9 %copy-start.38 = (f32[64]{0:T(128)S(1)}, f32[64]{0:T(128)}, u32[]{:S(2)}) copy-start(f32[64]{0:T(128)} %add_rsqrt_fusion.1) | copy-start | bytes 772
  177.1 5.5 %collective-permute-start.6 = (bf16[64,1,8,128]{3,0,2,1:T(8,128)(2,1)S(1)}, bf16[64,1,8,128]{3,0,2,1:T(8,128)(2,1)S(1)}, u32[]{:S(2)}, u32[]{:S(2)}) collective-permute-start(bf16[64,1,8,128]{3,0,2,1:T(8,128)(2,1)S(1)} %get-tuple-element.171), channel_id=1, source_target_pairs={{0,32},{32,64},{64,96},{96,128},{128,160},{160,192},{192,224},{224... | collective-permute-start | bytes 393224 | tf_op jit(solution)/shard_map/ppermute | solution.py:14
  178.4 4.1 %collective-permute-start.7 = (bf16[64,1,8,128]{3,0,2,1:T(8,128)(2,1)S(1)}, bf16[64,1,8,128]{3,0,2,1:T(8,128)(2,1)S(1)}, u32[]{:S(2)}, u32[]{:S(2)}) collective-permute-start(bf16[64,1,8,128]{3,0,2,1:T(8,128)(2,1)S(1)} %get-tuple-element.172), channel_id=1, source_target_pairs={{32,0},{64,32},{96,64},{128,96},{160,128},{192,160},{224,192},{0,2... | collective-permute-start | bytes 393224 | tf_op jit(solution)/shard_map/ppermute | solution.py:16
  182.6 10.5 %collective-permute-start.8 = (bf16[64,4,1,128]{3,0,2,1:T(8,128)(2,1)S(1)}, bf16[64,4,1,128]{3,0,2,1:T(8,128)(2,1)S(1)}, u32[]{:S(2)}, u32[]{:S(2)}) collective-permute-start(bf16[64,4,1,128]{3,0,2,1:T(8,128)(2,1)S(1)} %get-tuple-element.142), channel_id=1, source_target_pairs={{0,8},{8,16},{16,24},{24,0},{1,9},{9,17},{17,25},{25,1},{2,10},{10... | collective-permute-start | bytes 196616 | tf_op jit(solution)/shard_map/ppermute | solution.py:14
  186.6 6.4 %collective-permute-start.9 = (bf16[64,4,1,128]{3,0,2,1:T(8,128)(2,1)S(1)}, bf16[64,4,1,128]{3,0,2,1:T(8,128)(2,1)S(1)}, u32[]{:S(2)}, u32[]{:S(2)}) collective-permute-start(bf16[64,4,1,128]{3,0,2,1:T(8,128)(2,1)S(1)} %get-tuple-element.143), channel_id=1, source_target_pairs={{8,0},{16,8},{24,16},{0,24},{9,1},{17,9},{25,17},{1,25},{10,2},{18... | collective-permute-start | bytes 196616 | tf_op jit(solution)/shard_map/ppermute | solution.py:16
  195.1 6.6 %collective-permute-start.10 = (bf16[64,4,10,1]{0,2,3,1:T(8,128)(2,1)}, bf16[64,4,10,1]{0,2,3,1:T(8,128)(2,1)S(1)}, u32[]{:S(2)}, u32[]{:S(2)}) collective-permute-start(bf16[64,4,10,1]{0,2,3,1:T(8,128)(2,1)} %copy.162), channel_id=1, source_target_pairs={{0,1},{1,2},{2,3},{3,4},{4,5},{5,6},{6,7},{7,0},{8,9},{9,10},{10,1... | collective-permute-start | bytes 15368 | tf_op jit(solution)/shard_map/ppermute | solution.py:14
  197.6 4.7 %collective-permute-start.11 = (bf16[64,4,10,1]{0,2,3,1:T(8,128)(2,1)S(1)}, bf16[64,4,10,1]{0,2,3,1:T(8,128)(2,1)}, u32[]{:S(2)}, u32[]{:S(2)}) collective-permute-start(bf16[64,4,10,1]{0,2,3,1:T(8,128)(2,1)S(1)} %copy.163), channel_id=1, source_target_pairs={{1,0},{2,1},{3,2},{4,3},{5,4},{6,5},{7,6},{0,7},{9,8},{10,9},{11,1... | collective-permute-start | bytes 15368 | tf_op jit(solution)/shard_map/ppermute | solution.py:16
  201.1 2.3 %copy-start.8 = (bf16[64,4,1,128]{3,0,2,1:T(8,128)(2,1)S(1)}, bf16[64,4,1,128]{3,0,2,1:T(8,128)(2,1)}, u32[]{:S(2)}) copy-start(bf16[64,4,1,128]{3,0,2,1:T(8,128)(2,1)} %copy-done.7) | copy-start | bytes 196612
  210.6 1.1 copy-start.28
  211.1 0.8 copy-start.27
  211.6 0.8 copy-start.26
  212.3 0.8 copy-start.25
  212.7 0.8 copy-start.24
  213.4 0.8 copy-start.23
  213.8 0.8 copy-start.22
  214.5 0.8 copy-start.21
  214.9 0.8 copy-start.20
  215.8 1.8 copy-start.1
  (6 other events, 4.0 us)
Sparse Core Ops, SparseCore 0:
  31.4 120.7 all-reduce.2
where the time goes:
time: 229 us; the launch traced here: 224 us
  waiting for transfers between devices  106 us (46%)
  local copies, waits for them, and re-layouts  45 us (20%)
  starting transfers between devices  35.1 us (15%)
  between operations  15.1 us (7%)
  other arithmetic  15 us (7%)
  matrix products  8.25 us (4%)
    unnamed x2, waiting for transfers between devices  103 us
    ppermute x6, starting transfers between devices, extended(): lax.ppermute(head, axis, [((i + 1) % count, i) for i in range(count)])  20.8 us
    ppermute x6, starting transfers between devices, extended(): lax.ppermute(tail, axis, [(i, (i + 1) % count) for i in range(count)])  14.3 us
    unnamed x93, local copies, waits for them, and re-layouts  12.3 us
    transpose x20, local copies, waits for them, and re-layouts, convolve(): matrix = modulated[first_offset:first_offset + 3].transpose(1, 0, 2).resh...  11.6 us
    concatenate x18, local copies, waits for them, and re-layouts, convolve(): jnp.concatenate([padded[:, offset_x:offset_x + out_x, offset_y:offset_y +...  9.22 us
    dot_general x18, matrix products, convolve(): jnp.dot(matrix, stacked, preferred_element_type=jnp.float32)  5.18 us
  transfers between devices with their start and end apart: 13, of which 5 were waited for; matrix products, arithmetic and copies ran while one was open for 15% of the time, Pallas kernels for 0%

commit v1 on v0

v1 whole, which is shorter than its diff:
```python
import functools

import jax
import jax.numpy as jnp
from jax import lax
from jax.experimental import pallas as pl
from jax.experimental.pallas import tpu as pltpu
from jax.sharding import PartitionSpec as P

MESH = pl.DeviceIdType.MESH
F32 = jnp.float32
BF16 = jnp.bfloat16
NT = (((1,), (1,)), ((), ()))
SIDES = [(da, db, dc) for da in (0, -1, 1) for db in (0, -1, 1) for dc in (-1, 1)]
PLANAR = [(1, 0), (-1, 0), (0, 1), (0, -1), (1, 1), (1, -1), (-1, 1), (-1, -1)]


def shifted(sizes, me, move):
    return tuple((m + d + n) % n for m, d, n in zip(me, move, sizes))


def column(row):
    n = row.shape[1]
    eye = lax.broadcasted_iota(jnp.int32, (n, n), 0) == lax.broadcasted_iota(jnp.int32, (n, n), 1)
    return jnp.sum(jnp.where(eye, jnp.broadcast_to(row, (n, n)), 0.0), axis=1, keepdims=True)


def modulate(kernel_ref, style, affine_ref, main_ref, edge_ref):
    styles = (
        jnp.dot(style, affine_ref[...], precision=lax.Precision.HIGHEST, preferred_element_type=F32)
        + 1.0
    )
    total = jnp.zeros((64, 64), F32)
    for k in range(27):
        scaled = kernel_ref[k].astype(F32) * styles
        total = total + scaled * scaled
    demod = lax.rsqrt(jnp.sum(total, axis=1, keepdims=True) + 1e-08)

    def tap(k):
        return kernel_ref[k].astype(F32) * styles * demod

    zero = jnp.zeros((64, 64), F32)
    for g in range(3):
        for pair in range(5):
            left = tap(6 * pair + g)
            right = tap(6 * pair + 3 + g) if pair < 4 else zero
            main_ref[pl.ds(64 * g, 64), pl.ds(128 * pair, 128)] = jnp.concatenate(
                [left, right], axis=1
            ).astype(BF16)
    for ef in range(9):
        edge_ref[pl.ds(0, 64), pl.ds(128 * ef, 128)] = jnp.concatenate(
            [zero, tap(3 * ef)], axis=1
        ).astype(BF16)
        edge_ref[pl.ds(64, 64), pl.ds(128 * ef, 128)] = jnp.concatenate(
            [tap(3 * ef + 2), zero], axis=1
        ).astype(BF16)


def pack_edges(cells_ref, pick, edge_ref):
    rows = jnp.concatenate([cells_ref[1 + r // 8, 1 + r % 8] for r in range(16)], axis=1)
    both = lax.dot_general(pick, rows, NT, preferred_element_type=F32)
    edge_ref[...] = jnp.concatenate([both[:16], both[16:]], axis=1).astype(BF16)


def halo_copies(sizes, me, cells_ref, edge_ref, got_ref, sems):
    planar_send, planar_recv, edge_send, edge_recv = sems
    copies = []
    for n, (da, db) in enumerate(PLANAR):
        src_x = {1: pl.ds(2, 1), -1: pl.ds(1, 1), 0: pl.ds(1, 2)}[da]
        dst_x = {1: pl.ds(0, 1), -1: pl.ds(3, 1), 0: pl.ds(1, 2)}[da]
        src_y = {1: pl.ds(8, 1), -1: pl.ds(1, 1), 0: pl.ds(1, 8)}[db]
        dst_y = {1: pl.ds(0, 1), -1: pl.ds(9, 1), 0: pl.ds(1, 8)}[db]
        copies.append(
            pltpu.make_async_remote_copy(
                src_ref=cells_ref.at[src_x, src_y],
                dst_ref=cells_ref.at[dst_x, dst_y],
                send_sem=planar_send.at[n],
                recv_sem=planar_recv.at[n],
                device_id=shifted(sizes, me, (da, db, 0)),
                device_id_type=MESH,
            )
        )
    edges = [
        pltpu.make_async_remote_copy(
            src_ref=edge_ref,
            dst_ref=got_ref.at[n],
            send_sem=edge_send,
            recv_sem=edge_recv,
            device_id=shifted(sizes, me, move),
            device_id_type=MESH,
        )
        for n, move in enumerate(SIDES)
    ]
    return copies, edges


def wait_edges(got_ref, sem):
    pltpu.make_async_copy(got_ref, got_ref, sem).wait()


def unpack_edges(got_ref, ring_ref):
    lane = lax.broadcasted_iota(jnp.int32, (16, 128), 1)
    for da in (0, -1, 1):
        for db in (0, -1, 1):
            low = got_ref[SIDES.index((da, db, 1))].astype(F32)
            high = got_ref[SIDES.index((da, db, -1))].astype(F32)
            tile = jnp.where(lane < 64, high, low)
            for x in {0: (0, 1), 1: (1,), -1: (0,)}[da]:
                to_x = {0: 1 + x, 1: 0, -1: 3}[da]
                if db == 0:
                    ring_ref[to_x, pl.ds(1, 8)] = tile[8 * x : 8 * x + 8]
                elif db == 1:
                    ring_ref[to_x, pl.ds(0, 1)] = tile[8 * x + 7 : 8 * x + 8]
                else:
                    ring_ref[to_x, pl.ds(9, 1)] = tile[8 * x : 8 * x + 1]


def convolve(cells_ref, ring_ref, main_ref, edge_ref, emit):
    window = jnp.concatenate(
        [
            jnp.concatenate([ring_ref[e + x, pl.ds(f, 8)] for x in range(2)], axis=0)
            for e in range(3)
            for f in range(3)
        ],
        axis=1,
    ).astype(BF16)
    ends = lax.dot_general(edge_ref[...], window, NT, preferred_element_type=F32)
    lane = lax.broadcasted_iota(jnp.int32, (64, 128), 1)
    zero = jnp.zeros((64, 256), BF16)
    for pair in range(8):
        x, y = pair // 4, 2 * (pair % 4)
        stacked = jnp.concatenate(
            [
                jnp.concatenate([cells_ref[x + e, y + f], cells_ref[x + e, y + f + 1]], axis=1)
                for e in range(3)
                for f in range(3)
            ]
            + [zero],
            axis=0,
        )
        parts = jnp.dot(main_ref[...], stacked, preferred_element_type=F32)
        for half in range(2):
            row = 8 * x + y + half
            lanes = slice(128 * half, 128 * half + 128)
            low = jnp.where(
                lane == 0, ends[0:64, row : row + 1], pltpu.roll(parts[0:64, lanes], 1, 1)
            )
            high = jnp.where(
                lane == 127, ends[64:128, row : row + 1], pltpu.roll(parts[128:192, lanes], 127, 1)
            )
            emit(row, low + parts[64:128, lanes] + high)


def activate(values):
    return jnp.maximum(values, 0.2 * values) * jnp.sqrt(F32(2.0))


def paint(dest_ref, cell_ref, mass_ref, live_ref, left_ref, right_ref, part_ref):
    block = lax.broadcasted_iota(jnp.int32, (32, 64), 0)
    mass = jnp.where(block < live_ref[0], mass_ref[...].astype(F32), 0.0)
    key = dest_ref[...] * 2048 + cell_ref[...]
    key = jnp.concatenate([key[:16], key[16:]], axis=1)
    mass = jnp.concatenate([mass[:16], mass[16:]], axis=1)
    upper = key >> 7
    lower = key & 127
    tall = lax.broadcasted_iota(jnp.int32, (512, 128), 0)
    short = lax.broadcasted_iota(jnp.int32, (128, 128), 0)
    for n in range(16):
        lanes = pl.ds(128 * n, 128)
        left_ref[:, lanes] = jnp.where(
            tall == upper[n : n + 1], jnp.broadcast_to(mass[n : n + 1], (512, 128)), 0.0
        ).astype(BF16)
        right_ref[:, lanes] = jnp.where(short == lower[n : n + 1], 1.0, 0.0).astype(BF16)
    painted = lax.dot_general(left_ref[...], right_ref[...], NT, preferred_element_type=F32)
    part_ref[...] = painted.astype(BF16).reshape(32, 16, 128)


def body(
    sizes,
    features_ref,
    dest_ref,
    cell_ref,
    mass_ref,
    live_ref,
    style_ref,
    affine_first_ref,
    kernel_first_ref,
    bias_first_ref,
    gain_first_ref,
    affine_second_ref,
    kernel_second_ref,
    bias_second_ref,
    gain_second_ref,
    out_ref,
    left_ref,
    right_ref,
    part_ref,
    sums_ref,
    cells_first,
    cells_second,
    edge_first,
    edge_second,
    got_first,
    got_second,
    ring_ref,
    main_first,
    main_second,
    ends_first,
    ends_second,
    linear_ref,
    part_send,
    part_recv,
    planar_send,
    planar_recv,
    edge_send,
    edge_recv,
):
    n_gx, n_gy, n_gz = sizes
    slab = n_gy * n_gz
    me = (lax.axis_index("gx"), lax.axis_index("gy"), lax.axis_index("gz"))
    mine = me[1] * n_gz + me[2]

    def peer(j):
        other = (mine + j) % slab
        return other, (me[0], other // n_gz, other % n_gz)

    barrier = pltpu.get_barrier_semaphore()

    def greet(j, carry):
        pl.semaphore_signal(barrier, inc=1, device_id=peer(j)[1], device_id_type=MESH)
        return carry

    lax.fori_loop(1, slab, greet, 0)

    def greet_far(j, carry):
        move = (2 * (j // 9) - 1, (j // 3) % 3 - 1, j % 3 - 1)
        pl.semaphore_signal(
            barrier, inc=1, device_id=shifted(sizes, me, move), device_id_type=MESH
        )
        return carry

    lax.fori_loop(0, 18, greet_far, 0)

    for x in range(2):
        cells_first[1 + x, pl.ds(1, 8)] = features_ref[x]
    which = lax.broadcasted_iota(jnp.int32, (32, 2048), 0)
    place = lax.broadcasted_iota(jnp.int32, (32, 2048), 1)
    wanted = (which % 16) * 128 + (which // 16) * 127
    pick = jnp.where(place == wanted, 1.0, 0.0).astype(BF16)
    pack_edges(cells_first, pick, edge_first)
    paint(dest_ref, cell_ref, mass_ref, live_ref, left_ref, right_ref, part_ref)
    sums_ref[pl.ds(mine, 1)] = part_ref[pl.ds(mine, 1)]

    pl.semaphore_wait(barrier, slab - 1 + 18)

    def send_part(j, carry):
        other, device = peer(j)
        pltpu.make_async_remote_copy(
            src_ref=part_ref.at[other],
            dst_ref=sums_ref.at[mine],
            send_sem=part_send,
            recv_sem=part_recv,
            device_id=device,
            device_id_type=MESH,
        ).start()
        return carry

    lax.fori_loop(1, slab, send_part, 0)
    sems_first = (planar_send.at[0], planar_recv.at[0], edge_send.at[0], edge_recv.at[0])
    sems_second = (planar_send.at[1], planar_recv.at[1], edge_send.at[1], edge_recv.at[1])
    planar_one, edges_one = halo_copies(
        sizes, me, cells_first, edge_first, got_first, sems_first
    )
    for copy in planar_one + edges_one:
        copy.start()

    style = style_ref[...]
    modulate(kernel_first_ref, style, affine_first_ref, main_first, ends_first)
    modulate(kernel_second_ref, style, affine_second_ref, main_second, ends_second)
    bias_first = jnp.broadcast_to(column(bias_first_ref[...]), (64, 128))
    gain_first = jnp.broadcast_to(column(gain_first_ref[...]), (64, 128))
    bias_second = jnp.broadcast_to(column(bias_second_ref[...]), (64, 128))
    gain_second = jnp.broadcast_to(column(gain_second_ref[...]), (64, 128))

    for copy in planar_one:
        copy.wait()
    wait_edges(got_first, edge_recv.at[0])
    wait_edges(got_first, edge_send.at[0])
    unpack_edges(got_first, ring_ref)

    def keep(row, values):
        linear_ref[row] = values + bias_first

    convolve(cells_first, ring_ref, main_first, ends_first, keep)

    others = sums_ref.at[pl.ds(0, slab - 1)]
    pltpu.make_async_copy(others, others, part_recv).wait()
    pltpu.make_async_copy(others, others, part_send).wait()
    density = sums_ref[0].astype(F32)
    for n in range(1, slab):
        density = density + sums_ref[n].astype(F32)

    for row in range(16):
        values = linear_ref[row] + gain_first * density[row : row + 1]
        cells_second[1 + row // 8, 1 + row % 8] = activate(values).astype(BF16)
    pack_edges(cells_second, pick, edge_second)
    planar_two, edges_two = halo_copies(
        sizes, me, cells_second, edge_second, got_second, sems_second
    )
    for copy in planar_two + edges_two:
        copy.start()
    for copy in planar_two:
        copy.wait()
    wait_edges(got_second, edge_recv.at[1])
    wait_edges(got_second, edge_send.at[1])
    unpack_edges(got_second, ring_ref)

    def finish(row, values):
        out_ref[row // 8, row % 8] = activate(
            values + bias_second + gain_second * density[row : row + 1]
        ).astype(BF16)

    convolve(cells_second, ring_ref, main_second, ends_second, finish)


def shards(sizes, features, dest, cells, masses, live, style, *layers):
    slab = sizes[1] * sizes[2]
    affine_first, kernel_first, bias_first, gain_first = layers[:4]
    affine_second, kernel_second, bias_second, gain_second = layers[4:]
    vmem = pl.BlockSpec(memory_space=pltpu.VMEM)
    smem = pl.BlockSpec(memory_space=pltpu.SMEM)
    result = pl.pallas_call(
        functools.partial(body, sizes),
        out_shape=jax.ShapeDtypeStruct((2, 8, 64, 128), BF16),
        in_specs=[vmem] * 4 + [smem] + [vmem] * 9,
        out_specs=vmem,
        scratch_shapes=[
            pltpu.VMEM((512, 2048), BF16),
            pltpu.VMEM((128, 2048), BF16),
            pltpu.VMEM((slab, 16, 128), BF16),
            pltpu.VMEM((slab, 16, 128), BF16),
            pltpu.VMEM((4, 10, 64, 128), BF16),
            pltpu.VMEM((4, 10, 64, 128), BF16),
            pltpu.VMEM((16, 128), BF16),
            pltpu.VMEM((16, 128), BF16),
            pltpu.VMEM((18, 16, 128), BF16),
            pltpu.VMEM((18, 16, 128), BF16),
            pltpu.VMEM((4, 16, 128), F32),
            pltpu.VMEM((192, 640), BF16),
            pltpu.VMEM((192, 640), BF16),
            pltpu.VMEM((128, 1152), BF16),
            pltpu.VMEM((128, 1152), BF16),
            pltpu.VMEM((16, 64, 128), F32),
            pltpu.SemaphoreType.DMA,
            pltpu.SemaphoreType.DMA,
            pltpu.SemaphoreType.DMA((2, 8)),
            pltpu.SemaphoreType.DMA((2, 8)),
            pltpu.SemaphoreType.DMA((2,)),
            pltpu.SemaphoreType.DMA((2,)),
        ],
        compiler_params=pltpu.CompilerParams(
            collective_id=0, has_side_effects=True, vmem_limit_bytes=40 * 1024 * 1024
        ),
        name="styled_block",
    )(
        features.transpose(1, 2, 0, 3),
        dest,
        cells,
        masses,
        live,
        style.reshape(1, -1),
        affine_first,
        kernel_first,
        bias_first.reshape(1, -1),
        gain_first.reshape(1, -1),
        affine_second,
        kernel_second,
        bias_second.reshape(1, -1),
        gain_second.reshape(1, -1),
    )
    return result.transpose(2, 0, 1, 3)


def solution(mesh):
    sizes = (mesh.shape["gx"], mesh.shape["gy"], mesh.shape["gz"])
    spread = P(("gx", "gy", "gz"), None)
    return jax.shard_map(
        functools.partial(shards, sizes),
        mesh=mesh,
        in_specs=(P(None, "gx", "gy", "gz"), spread, spread, spread, P(("gx", "gy", "gz")))
        + (P(),) * 9,
        out_specs=P(None, "gx", "gy", "gz"),
        check_vma=False,
    )
```

time: 229 us -> 38.6 us (0.17); the launches traced: 224 us -> 38.4 us
  waiting for transfers between devices: 106 us -> 0 us
  local copies, waits for them, and re-layouts: 45 us -> 3.65 us
  starting transfers between devices: 35.1 us -> 0 us
  Pallas kernels: 0 us -> 34 us
  other arithmetic: 15 us -> 0 us
  between operations: 15.1 us -> 0.81 us
  matrix products: 8.25 us -> 0 us
    unnamed x2 -> x0, waiting for transfers between devices: 103 us -> none
    ppermute x12 -> x0, starting transfers between devices: 35.1 us -> none  [the longest x6 20.8 us: extended(): lax.ppermute(head, axis, [((i + 1) % count, i) for i in range(count)])]
    pallas_call x0 -> x1, Pallas kernels: none -> 34 us  [shards(): pl.pallas_call(functools.partial(body, sizes), out_shape=jax.ShapeDtypeSt...]
    transpose x20 -> x1, local copies, waits for them, and re-layouts: 11.6 us -> 0.88 us  [shards(): return result.transpose(2, 0, 1, 3)]
    unnamed x93 -> x28, local copies, waits for them, and re-layouts: 12.3 us -> 2.77 us
    concatenate x19 -> x0, local copies, waits for them, and re-layouts: 9.24 us -> none  [the longest x18 9.22 us: convolve(): jnp.concatenate([padded[:, offset_x:offset_x + out_x, offset_y:offset_y +...]
    dot_general x25 -> x0, matrix products: 8.25 us -> none  [the longest x18 5.18 us: convolve(): jnp.dot(matrix, stacked, preferred_element_type=jnp.float32)]
    concatenate x19 -> x0, other arithmetic: 4.97 us -> none  [the longest x6 3.58 us: extended(): jnp.concatenate([lax.ppermute(tail, axis, [(i, (i + 1) % count) for i in...]
  transfers between devices with their start and end apart: 13 -> 0, of which waited for: 5 -> 0; matrix products, arithmetic and copies ran while one was open for 15% -> 0% of each run, Pallas kernels for 0% -> 0%
where the time goes in v1:
time: 38.6 us; the launch traced here: 38.4 us
  Pallas kernels  34 us (88%)
  local copies, waits for them, and re-layouts  3.65 us (9%)
  between operations  0.81 us (2%)
    pallas_call x1, Pallas kernels, shards(): pl.pallas_call(functools.partial(body, sizes), out_shape=jax.ShapeDtypeSt...  34 us
    unnamed x28, local copies, waits for them, and re-layouts  2.77 us
    transpose x1, local copies, waits for them, and re-layouts, shards(): return result.transpose(2, 0, 1, 3)  0.88 us

profile of v1, /device:TPU:1, one launch (start us, length us, event | category | flops | bytes accessed | tf_op | source)
XLA Modules:
  0.0 38.4 jit_solution(5716927226223729694)
XLA Ops:
  0.7 0.0 copy-start.11
  0.7 0.6 %copy-done.11 = s32[32,1]{0,1:T(1,128)S(1)} copy-done((s32[32,1]{0,1:T(1,128)S(1)}, s32[32,1]{0,1:T(1,128)}, u32[]{:S(2)}) %copy-start.11) | copy-done | bytes 152
  1.3 0.0 copy-start.9
  1.3 0.1 copy.16.dest_ref
  1.4 0.0 copy-start.10
  1.4 0.0 copy-start.1
  1.4 1.1 %copy.21 = bf16[64,2,8,128]{3,0,2,1:T(8,128)(2,1)S(1)} copy(bf16[64,2,8,128]{3,2,1,0:T(8,128)(2,1)} %param.14) | data formatting | bytes 524288 | tf_op args[0]
  2.5 0.0 copy-start
  2.5 0.0 copy-done.9
  2.5 0.1 copy.17.affine_first_ref
  2.6 0.0 copy-done.10
  2.6 0.0 copy-start.2
  2.7 0.0 copy-start.3
  2.7 0.0 copy-start.4
  2.7 0.0 copy-start.5
  2.7 0.0 copy-start.6
  2.7 0.0 copy-start.7
  2.7 0.0 copy-start.8
  2.7 0.1 copy.18.affine_second_ref
  2.9 0.0 copy-done.1
  2.9 0.7 %copy-done = bf16[27,64,64]{2,1,0:T(8,128)(2,1)S(1)} copy-done((bf16[27,64,64]{2,1,0:T(8,128)(2,1)S(1)}, bf16[27,64,64]{2,1,0:T(8,128)(2,1)}, u32[]{:S(2)}) %copy-start) | copy-done | bytes 221208
  3.5 0.0 copy-done.2
  3.5 0.0 copy-done.3
  3.5 0.0 copy-done.4
  3.5 0.0 copy-done.5
  3.5 0.0 copy-done.6
  3.5 0.0 copy-done.7
  3.6 0.0 copy-done.8
  3.6 34.0 %styled_block.1 = bf16[2,8,64,128]{3,2,1,0:T(8,128)(2,1)S(1)} custom-call(bf16[2,8,64,128]{3,2,1,0:T(8,128)(2,1)S(1)} %bitcast.10, s32[32,1]{1,0:T(8,128)S(1)} %copy.16.dest_ref, s32[32,64]{1,0:T(8,128)S(1)} %copy-done.2, bf16[32,64]{1,0:T(8,128)(2,1)S(1)} %copy-done.3, s32[1]{0:T(128)S(6)} %copy.22.live_ref, f32[1,512]{1,0:T(1,128)S(1)} %bitcast.11, ...), custom_call_target="tpu_custom_call" | custom-call | tf_op jit(solution)/shard_map/styled_block/pallas_call | solution.py:332
  37.6 0.9 %copy.19 = bf16[64,2,8,128]{3,2,1,0:T(8,128)(2,1)} copy(bf16[64,2,8,128]{3,0,2,1:T(8,128)(2,1)S(1)} %bitcast.9) | data formatting | bytes 524288 | tf_op jit(solution)/shard_map/transpose | solution.py:381
Async XLA Ops:
  0.7 0.7 %copy-start.11 = (s32[32,1]{0,1:T(1,128)S(1)}, s32[32,1]{0,1:T(1,128)}, u32[]{:S(2)}) copy-start(s32[32,1]{0,1:T(1,128)} %param.15) | copy-start | bytes 388
  1.3 1.2 %copy-start.9 = (f32[512,64]{0,1:T(8,128)S(1)}, f32[512,64]{0,1:T(8,128)}, u32[]{:S(2)}) copy-start(f32[512,64]{0,1:T(8,128)} %param.20) | copy-start | bytes 393220
  1.4 1.2 %copy-start.10 = (f32[512,64]{0,1:T(8,128)S(1)}, f32[512,64]{0,1:T(8,128)}, u32[]{:S(2)}) copy-start(f32[512,64]{0,1:T(8,128)} %param.24) | copy-start | bytes 393220
  1.4 1.5 %copy-start.1 = (bf16[27,64,64]{2,1,0:T(8,128)(2,1)S(1)}, bf16[27,64,64]{2,1,0:T(8,128)(2,1)}, u32[]{:S(2)}) copy-start(bf16[27,64,64]{2,1,0:T(8,128)(2,1)} %kernel_second_ref.1) | copy-start | bytes 663556
  2.5 1.0 %copy-start = (bf16[27,64,64]{2,1,0:T(8,128)(2,1)S(1)}, bf16[27,64,64]{2,1,0:T(8,128)(2,1)}, u32[]{:S(2)}) copy-start(bf16[27,64,64]{2,1,0:T(8,128)(2,1)} %kernel_first_ref.1) | copy-start | bytes 663556
  2.6 0.9 %copy-start.2 = (s32[32,64]{1,0:T(8,128)S(1)}, s32[32,64]{1,0:T(8,128)}, u32[]{:S(2)}) copy-start(s32[32,64]{1,0:T(8,128)} %cell_ref.1) | copy-start | bytes 24580
  2.7 0.9 %copy-start.3 = (bf16[32,64]{1,0:T(8,128)(2,1)S(1)}, bf16[32,64]{1,0:T(8,128)(2,1)}, u32[]{:S(2)}) copy-start(bf16[32,64]{1,0:T(8,128)(2,1)} %mass_ref.1) | copy-start | bytes 12292
  2.7 0.9 %copy-start.4 = (f32[512]{0:T(512)S(1)}, f32[512]{0:T(512)}, u32[]{:S(2)}) copy-start(f32[512]{0:T(512)} %param.19) | copy-start | bytes 6148
  2.7 0.8 %copy-start.5 = (f32[64]{0:T(128)S(1)}, f32[64]{0:T(128)}, u32[]{:S(2)}) copy-start(f32[64]{0:T(128)} %param.22) | copy-start | bytes 772
  2.7 0.8 %copy-start.6 = (f32[64]{0:T(128)S(1)}, f32[64]{0:T(128)}, u32[]{:S(2)}) copy-start(f32[64]{0:T(128)} %param.23) | copy-start | bytes 772
  2.7 0.8 %copy-start.7 = (f32[64]{0:T(128)S(1)}, f32[64]{0:T(128)}, u32[]{:S(2)}) copy-start(f32[64]{0:T(128)} %param.26) | copy-start | bytes 772
  2.7 0.8 %copy-start.8 = (f32[64]{0:T(128)S(1)}, f32[64]{0:T(128)}, u32[]{:S(2)}) copy-start(f32[64]{0:T(128)} %param.27) | copy-start | bytes 772

commit v2 on v1

v2 whole, which is shorter than its diff:
```python
import functools

import jax
import jax.numpy as jnp
from jax import lax
from jax.experimental import pallas as pl
from jax.experimental.pallas import tpu as pltpu
from jax.sharding import PartitionSpec as P

MESH = pl.DeviceIdType.MESH
F32 = jnp.float32
BF16 = jnp.bfloat16
NT = (((1,), (1,)), ((), ()))
SIDES = [(da, db, dc) for da in (-1, 1, 0) for db in (-1, 1, 0) for dc in (-1, 1)]
PLANAR = [(1, 1), (1, -1), (-1, 1), (-1, -1), (0, 1), (0, -1), (1, 0), (-1, 0)]


def column(row):
    n = row.shape[1]
    eye = lax.broadcasted_iota(jnp.int32, (n, n), 0) == lax.broadcasted_iota(jnp.int32, (n, n), 1)
    return jnp.sum(jnp.where(eye, jnp.broadcast_to(row, (n, n)), 0.0), axis=1, keepdims=True)


def modulate(kernel_ref, style, affine, main_ref, edge_ref):
    styles = (
        lax.dot_general(
            style, affine, NT, precision=lax.Precision.HIGHEST, preferred_element_type=F32
        )
        + 1.0
    )
    total = jnp.zeros((64, 64), F32)
    for k in range(27):
        scaled = kernel_ref[k].astype(F32) * styles
        total = total + scaled * scaled
    demod = lax.rsqrt(jnp.sum(total, axis=1, keepdims=True) + 1e-08)

    def tap(k):
        return kernel_ref[k].astype(F32) * styles * demod

    zero = jnp.zeros((64, 64), F32)
    for g in range(3):
        for e in range(3):
            for half in range(2):
                k = 9 * e + 6 * half + g
                right = zero if half else tap(k + 3)
                main_ref[pl.ds(64 * g, 64), pl.ds(256 * e + 128 * half, 128)] = jnp.concatenate(
                    [tap(k), right], axis=1
                ).astype(BF16)
    for ef in range(9):
        edge_ref[pl.ds(0, 64), pl.ds(128 * ef, 128)] = jnp.concatenate(
            [zero, tap(3 * ef)], axis=1
        ).astype(BF16)
        edge_ref[pl.ds(64, 64), pl.ds(128 * ef, 128)] = jnp.concatenate(
            [tap(3 * ef + 2), zero], axis=1
        ).astype(BF16)


def pack_edges(cells_ref, pick, edge_ref):
    rows = jnp.concatenate([cells_ref[1 + r // 8, 1 + r % 8] for r in range(16)], axis=1)
    both = lax.dot_general(pick, rows, NT, preferred_element_type=F32)
    edge_ref[...] = jnp.concatenate([both[:16], both[16:]], axis=1).astype(BF16)


def unpack_edges(got_ref, ring_ref):
    lane = lax.broadcasted_iota(jnp.int32, (16, 128), 1)
    for da in (0, -1, 1):
        for db in (0, -1, 1):
            low = got_ref[SIDES.index((da, db, 1))].astype(F32)
            high = got_ref[SIDES.index((da, db, -1))].astype(F32)
            tile = jnp.where(lane < 64, high, low)
            for x in {0: (0, 1), 1: (1,), -1: (0,)}[da]:
                to_x = {0: 1 + x, 1: 0, -1: 3}[da]
                if db == 0:
                    ring_ref[to_x, pl.ds(1, 8)] = tile[8 * x : 8 * x + 8]
                elif db == 1:
                    ring_ref[to_x, pl.ds(0, 1)] = tile[8 * x + 7 : 8 * x + 8]
                else:
                    ring_ref[to_x, pl.ds(9, 1)] = tile[8 * x : 8 * x + 1]


def stack(cells_ref, plane, y):
    zero = jnp.zeros((64, 256), BF16)
    return jnp.concatenate(
        [
            jnp.concatenate([cells_ref[plane, y + f], cells_ref[plane, y + f + 1]], axis=1)
            for f in range(3)
        ]
        + [zero],
        axis=0,
    )


def taps(main_ref, e, stacked):
    return jnp.dot(main_ref[:, pl.ds(256 * e, 256)], stacked, preferred_element_type=F32)


def convolve_own(cells_ref, main_ref, parts_ref):
    for pair in range(4):
        near = stack(cells_ref, 1, 2 * pair)
        far = stack(cells_ref, 2, 2 * pair)
        parts_ref[pair] = taps(main_ref, 1, near) + taps(main_ref, 2, far)
        parts_ref[4 + pair] = taps(main_ref, 0, near) + taps(main_ref, 1, far)


def convolve_halo(cells_ref, ring_ref, main_ref, edge_ref, parts_ref, emit):
    window = jnp.concatenate(
        [
            jnp.concatenate([ring_ref[e + x, pl.ds(f, 8)] for x in range(2)], axis=0)
            for e in range(3)
            for f in range(3)
        ],
        axis=1,
    ).astype(BF16)
    ends = lax.dot_general(edge_ref[...], window, NT, preferred_element_type=F32)
    lane = lax.broadcasted_iota(jnp.int32, (64, 128), 1)
    for pair in range(8):
        x, y = pair // 4, 2 * (pair % 4)
        parts = parts_ref[pair] + taps(main_ref, 2 * x, stack(cells_ref, 3 * x, y))
        for half in range(2):
            row = 8 * x + y + half
            lanes = slice(128 * half, 128 * half + 128)
            low = jnp.where(
                lane == 0, ends[0:64, row : row + 1], pltpu.roll(parts[0:64, lanes], 1, 1)
            )
            high = jnp.where(
                lane == 127, ends[64:128, row : row + 1], pltpu.roll(parts[128:192, lanes], 127, 1)
            )
            emit(row, low + parts[64:128, lanes] + high)


def activate(values):
    return jnp.maximum(values, 0.2 * values) * jnp.sqrt(F32(2.0))


def paint(dest, cells, mass, live, left_ref, right_ref, part_ref):
    block = lax.broadcasted_iota(jnp.int32, (32, 64), 0)
    mass = jnp.where(block < jnp.broadcast_to(live, (32, 64)), mass.astype(F32), 0.0)
    n = dest.shape[1]
    eye = lax.broadcasted_iota(jnp.int32, (n, n), 0) == lax.broadcasted_iota(jnp.int32, (n, n), 1)
    spread = jnp.where(eye, jnp.broadcast_to(dest.astype(F32), (n, n)), 0.0)
    base = jnp.sum(spread, axis=1, keepdims=True).astype(jnp.int32)
    key = base * 2048 + cells
    key = jnp.concatenate([key[:16], key[16:]], axis=1)
    mass = jnp.concatenate([mass[:16], mass[16:]], axis=1)
    upper = key >> 7
    lower = key & 127
    tall = lax.broadcasted_iota(jnp.int32, (512, 128), 0)
    short = lax.broadcasted_iota(jnp.int32, (128, 128), 0)
    for n in range(16):
        lanes = pl.ds(128 * n, 128)
        left_ref[:, lanes] = jnp.where(
            tall == upper[n : n + 1], jnp.broadcast_to(mass[n : n + 1], (512, 128)), 0.0
        ).astype(BF16)
        right_ref[:, lanes] = jnp.where(short == lower[n : n + 1], 1.0, 0.0).astype(BF16)
    painted = lax.dot_general(left_ref[...], right_ref[...], NT, preferred_element_type=F32)
    part_ref[...] = painted.astype(BF16).reshape(32, 16, 128)


def body(sizes, n_in, *refs):
    sources = refs[:n_in]
    out_ref = refs[n_in]
    held = refs[n_in + 1 : 2 * n_in + 1]
    (
        left_ref,
        right_ref,
        part_ref,
        sums_ref,
        cells_first,
        cells_second,
        edge_first,
        edge_second,
        got_first,
        got_second,
        ring_ref,
        main_first,
        main_second,
        ends_first,
        ends_second,
        parts_ref,
        fetch_sem,
        part_sem,
        halo_sem,
        edge_sem,
    ) = refs[2 * n_in + 1 :]
    n_gx, n_gy, n_gz = sizes
    slab = n_gy * n_gz
    me = (lax.axis_index("gx"), lax.axis_index("gy"), lax.axis_index("gz"))
    mine = me[1] * n_gz + me[2]
    at_x = {d: (me[0] + d + n_gx) % n_gx for d in (-1, 0, 1)}
    at_y = [(me[1] + d) % n_gy for d in range(n_gy)]
    at_z = [(me[2] + d) % n_gz for d in range(n_gz)]

    def place(move):
        return (at_x[move[0]], at_y[move[1] % n_gy], at_z[move[2] % n_gz])

    others = [(dy, dz) for dy in range(n_gy) for dz in range(n_gz) if (dy, dz) != (0, 0)]

    fetches = [
        pltpu.make_async_copy(source, kept, fetch_sem.at[n])
        for n, (source, kept) in enumerate(zip(sources, held))
    ]
    for fetch in fetches[:5]:
        fetch.start()
    barrier = pltpu.get_barrier_semaphore()
    for dy, dz in others:
        pl.semaphore_signal(
            barrier, inc=1, device_id=(me[0], at_y[dy], at_z[dz]), device_id_type=MESH
        )
    for da in (-1, 1):
        for db in (-1, 0, 1):
            for dc in (-1, 0, 1):
                pl.semaphore_signal(
                    barrier, inc=1, device_id=place((da, db, dc)), device_id_type=MESH
                )
    for fetch in fetches[5:]:
        fetch.start()

    dest, cells, mass, live, features, style, *layers = held
    for fetch in fetches[:4]:
        fetch.wait()
    paint(dest[...], cells[...], mass[...], live[...].reshape(1, 1), left_ref, right_ref, part_ref)
    sums_ref[pl.ds(mine, 1)] = part_ref[pl.ds(mine, 1)]

    which = lax.broadcasted_iota(jnp.int32, (32, 2048), 0)
    spot = lax.broadcasted_iota(jnp.int32, (32, 2048), 1)
    wanted = (which % 16) * 128 + (which // 16) * 127
    pick = jnp.where(spot == wanted, 1.0, 0.0).astype(BF16)

    fetches[4].wait()
    for x in range(2):
        turned = jnp.transpose(features[:, x].astype(F32), (1, 0, 2))
        cells_first[1 + x, pl.ds(1, 8)] = turned.astype(BF16)
    pack_edges(cells_first, pick, edge_first)

    pl.semaphore_wait(barrier, slab - 1 + 18)

    for dy, dz in others:
        pltpu.make_async_remote_copy(
            src_ref=part_ref.at[at_y[dy] * n_gz + at_z[dz]],
            dst_ref=sums_ref.at[mine],
            send_sem=part_sem.at[0],
            recv_sem=part_sem.at[1],
            device_id=(me[0], at_y[dy], at_z[dz]),
            device_id_type=MESH,
        ).start()

    def start_halo(layer, cells_ref, edge_ref, got_ref):
        for n, move in enumerate(SIDES):
            pltpu.make_async_remote_copy(
                src_ref=edge_ref,
                dst_ref=got_ref.at[n],
                send_sem=edge_sem.at[layer, 0],
                recv_sem=edge_sem.at[layer, 1],
                device_id=place(move),
                device_id_type=MESH,
            ).start()
        for da, db in PLANAR:
            group = 0 if da == 0 else 2
            src_x = {1: pl.ds(2, 1), -1: pl.ds(1, 1), 0: pl.ds(1, 2)}[da]
            dst_x = {1: pl.ds(0, 1), -1: pl.ds(3, 1), 0: pl.ds(1, 2)}[da]
            src_y = {1: pl.ds(8, 1), -1: pl.ds(1, 1), 0: pl.ds(1, 8)}[db]
            dst_y = {1: pl.ds(0, 1), -1: pl.ds(9, 1), 0: pl.ds(1, 8)}[db]
            pltpu.make_async_remote_copy(
                src_ref=cells_ref.at[src_x, src_y],
                dst_ref=cells_ref.at[dst_x, dst_y],
                send_sem=halo_sem.at[layer, group],
                recv_sem=halo_sem.at[layer, group + 1],
                device_id=place((da, db, 0)),
                device_id_type=MESH,
            ).start()

    def wait_for(ref, sem):
        pltpu.make_async_copy(ref, ref, sem).wait()

    def wait_beside(layer, cells_ref):
        four = cells_ref.at[pl.ds(0, 1), pl.ds(0, 4)]
        for sem in range(2):
            wait_for(four, halo_sem.at[layer, sem])

    def wait_across(layer, cells_ref, got_ref):
        twenty = cells_ref.at[pl.ds(0, 2), pl.ds(0, 10)]
        for sem in range(2):
            wait_for(twenty, halo_sem.at[layer, 2 + sem])
            wait_for(got_ref, edge_sem.at[layer, sem])

    start_halo(0, cells_first, edge_first, got_first)

    for fetch in fetches[5:]:
        fetch.wait()
    style = style[...]
    modulate(layers[1], style, layers[0][...], main_first, ends_first)
    modulate(layers[5], style, layers[4][...], main_second, ends_second)
    bias_first, gain_first, bias_second, gain_second = (
        jnp.broadcast_to(column(layers[n][...]), (64, 128)) for n in (2, 3, 6, 7)
    )

    wait_beside(0, cells_first)
    convolve_own(cells_first, main_first, parts_ref)
    rest = sums_ref.at[pl.ds(0, slab - 1)]
    wait_for(rest, part_sem.at[1])
    wait_for(rest, part_sem.at[0])
    density = sums_ref[0].astype(F32)
    for n in range(1, slab):
        density = density + sums_ref[n].astype(F32)
    wait_across(0, cells_first, got_first)
    unpack_edges(got_first, ring_ref)

    def keep(row, values):
        cells_second[1 + row // 8, 1 + row % 8] = activate(
            values + gain_first * density[row : row + 1] + bias_first
        ).astype(BF16)

    convolve_halo(cells_first, ring_ref, main_first, ends_first, parts_ref, keep)
    pack_edges(cells_second, pick, edge_second)
    start_halo(1, cells_second, edge_second, got_second)
    wait_beside(1, cells_second)
    convolve_own(cells_second, main_second, parts_ref)
    wait_across(1, cells_second, got_second)
    unpack_edges(got_second, ring_ref)

    def finish(row, values):
        out_ref[row // 8, row % 8] = activate(
            values + gain_second * density[row : row + 1] + bias_second
        ).astype(BF16)

    convolve_halo(cells_second, ring_ref, main_second, ends_second, parts_ref, finish)


def shards(sizes, features, dest, cells, masses, live, style, *layers):
    slab = sizes[1] * sizes[2]
    operands = [
        dest.reshape(1, -1),
        cells,
        masses,
        live,
        features,
        style.reshape(1, -1),
    ]
    for affine, kernel, bias, gain in (layers[:4], layers[4:]):
        operands += [affine.T, kernel, bias.reshape(1, -1), gain.reshape(1, -1)]
    result = pl.pallas_call(
        functools.partial(body, sizes, len(operands)),
        out_shape=jax.ShapeDtypeStruct((2, 8, 64, 128), BF16),
        in_specs=[pl.BlockSpec(memory_space=pltpu.HBM)] * len(operands),
        out_specs=pl.BlockSpec(memory_space=pltpu.VMEM),
        scratch_shapes=[pltpu.VMEM(x.shape, x.dtype) for x in operands]
        + [
            pltpu.VMEM((512, 2048), BF16),
            pltpu.VMEM((128, 2048), BF16),
            pltpu.VMEM((slab, 16, 128), BF16),
            pltpu.VMEM((slab, 16, 128), BF16),
            pltpu.VMEM((4, 10, 64, 128), BF16),
            pltpu.VMEM((4, 10, 64, 128), BF16),
            pltpu.VMEM((16, 128), BF16),
            pltpu.VMEM((16, 128), BF16),
            pltpu.VMEM((18, 16, 128), BF16),
            pltpu.VMEM((18, 16, 128), BF16),
            pltpu.VMEM((4, 16, 128), F32),
            pltpu.VMEM((192, 768), BF16),
            pltpu.VMEM((192, 768), BF16),
            pltpu.VMEM((128, 1152), BF16),
            pltpu.VMEM((128, 1152), BF16),
            pltpu.VMEM((8, 192, 256), F32),
            pltpu.SemaphoreType.DMA((len(operands),)),
            pltpu.SemaphoreType.DMA((2,)),
            pltpu.SemaphoreType.DMA((2, 4)),
            pltpu.SemaphoreType.DMA((2, 2)),
        ],
        compiler_params=pltpu.CompilerParams(
            collective_id=0, has_side_effects=True, vmem_limit_bytes=63 * 1024 * 1024
        ),
        name="styled_block",
    )(*operands)
    return result.transpose(2, 0, 1, 3)


def solution(mesh):
    sizes = (mesh.shape["gx"], mesh.shape["gy"], mesh.shape["gz"])
    spread = P(("gx", "gy", "gz"), None)
    return jax.shard_map(
        functools.partial(shards, sizes),
        mesh=mesh,
        in_specs=(P(None, "gx", "gy", "gz"), spread, spread, spread, P(("gx", "gy", "gz")))
        + (P(),) * 9,
        out_specs=P(None, "gx", "gy", "gz"),
        check_vma=False,
    )
```

time: 38.6 us -> 29.9 us (0.77)
  Pallas kernels: 34 us -> 27.3 us
  local copies, waits for them, and re-layouts: 3.65 us -> 1.83 us
    pallas_call x1, Pallas kernels: 34 us -> 27.3 us  [shards(): pl.pallas_call(functools.partial(body, sizes, len(operands)), out_shape=j...]
    unnamed x28 -> x0, local copies, waits for them, and re-layouts: 2.77 us -> none
    transpose x1, local copies, waits for them, and re-layouts: 0.88 us -> 1.83 us  [shards(): return result.transpose(2, 0, 1, 3)]
where the time goes in v2:
time: 29.9 us; the launch traced here: 29.8 us
  Pallas kernels  27.3 us (91%)
  local copies, waits for them, and re-layouts  1.83 us (6%)
  between operations  0.66 us (2%)
    pallas_call x1, Pallas kernels, shards(): pl.pallas_call(functools.partial(body, sizes, len(operands)), out_shape=j...  27.3 us
    transpose x1, local copies, waits for them, and re-layouts, shards(): return result.transpose(2, 0, 1, 3)  1.83 us

profile of v2, /device:TPU:1, one launch (start us, length us, event | category | flops | bytes accessed | tf_op | source)
XLA Modules:
  0.0 29.8 jit_solution(11103161152670036583)
XLA Ops:
  0.7 27.3 %styled_block.1 = bf16[2,8,64,128]{3,2,1,0:T(8,128)(2,1)} custom-call(s32[1,32]{1,0:T(1,128)} %bitcast.13, s32[32,64]{1,0:T(8,128)} %refs_1_.1, bf16[32,64]{1,0:T(8,128)(2,1)} %refs_2_.1, s32[1]{0:T(128)S(6)} %copy.16.refs_3_, bf16[64,2,8,128]{3,2,1,0:T(8,128)(2,1)} %refs_4_.1, f32[1,512]{1,0:T(1,128)} %bitcast.12, f32[64,512]{1,0:T(8,128)} %bitcast.10, ...), custom_call_target="tpu_custom_call" | custom-call | tf_op jit(solution)/shard_map/styled_block/pallas_call | solution.py:341
  28.0 1.8 %copy.15 = bf16[64,2,8,128]{3,2,1,0:T(8,128)(2,1)} copy(bf16[64,2,8,128]{3,0,2,1:T(8,128)(2,1)} %bitcast.9) | data formatting | bytes 524288 | tf_op jit(solution)/shard_map/transpose | solution.py:374

commit v3 on v2

--- a/solution.py
+++ b/solution.py
@@ -102,7 +102,7 @@
         parts_ref[4 + pair] = taps(main_ref, 0, near) + taps(main_ref, 1, far)
 
 
-def convolve_halo(cells_ref, ring_ref, main_ref, edge_ref, parts_ref, emit):
+def convolve_ends(ring_ref, edge_ref):
     window = jnp.concatenate(
         [
             jnp.concatenate([ring_ref[e + x, pl.ds(f, 8)] for x in range(2)], axis=0)
@@ -111,7 +111,10 @@
         ],
         axis=1,
     ).astype(BF16)
-    ends = lax.dot_general(edge_ref[...], window, NT, preferred_element_type=F32)
+    return lax.dot_general(edge_ref[...], window, NT, preferred_element_type=F32)
+
+
+def convolve_halo(cells_ref, ends, main_ref, parts_ref, emit):
     lane = lax.broadcasted_iota(jnp.int32, (64, 128), 1)
     for pair in range(8):
         x, y = pair // 4, 2 * (pair % 4)
@@ -134,7 +137,7 @@
 
 def paint(dest, cells, mass, live, left_ref, right_ref, part_ref):
     block = lax.broadcasted_iota(jnp.int32, (32, 64), 0)
-    mass = jnp.where(block < jnp.broadcast_to(live, (32, 64)), mass.astype(F32), 0.0)
+    mass = jnp.where(block < live, mass.astype(F32), 0.0)
     n = dest.shape[1]
     eye = lax.broadcasted_iota(jnp.int32, (n, n), 0) == lax.broadcasted_iota(jnp.int32, (n, n), 1)
     spread = jnp.where(eye, jnp.broadcast_to(dest.astype(F32), (n, n)), 0.0)
@@ -156,7 +159,7 @@
     part_ref[...] = painted.astype(BF16).reshape(32, 16, 128)
 
 
-def body(sizes, n_in, *refs):
+def body(sizes, n_in, live_ref, *refs):
     sources = refs[:n_in]
     out_ref = refs[n_in]
     held = refs[n_in + 1 : 2 * n_in + 1]
@@ -199,7 +202,7 @@
         pltpu.make_async_copy(source, kept, fetch_sem.at[n])
         for n, (source, kept) in enumerate(zip(sources, held))
     ]
-    for fetch in fetches[:5]:
+    for fetch in fetches[:4]:
         fetch.start()
     barrier = pltpu.get_barrier_semaphore()
     for dy, dz in others:
@@ -212,37 +215,22 @@
                 pl.semaphore_signal(
                     barrier, inc=1, device_id=place((da, db, dc)), device_id_type=MESH
                 )
-    for fetch in fetches[5:]:
+    for fetch in fetches[4:]:
         fetch.start()
 
-    dest, cells, mass, live, features, style, *layers = held
-    for fetch in fetches[:4]:
-        fetch.wait()
-    paint(dest[...], cells[...], mass[...], live[...].reshape(1, 1), left_ref, right_ref, part_ref)
-    sums_ref[pl.ds(mine, 1)] = part_ref[pl.ds(mine, 1)]
-
+    features, dest, cells, mass, style, *layers = held
     which = lax.broadcasted_iota(jnp.int32, (32, 2048), 0)
     spot = lax.broadcasted_iota(jnp.int32, (32, 2048), 1)
     wanted = (which % 16) * 128 + (which // 16) * 127
     pick = jnp.where(spot == wanted, 1.0, 0.0).astype(BF16)
 
-    fetches[4].wait()
+    fetches[0].wait()
     for x in range(2):
         turned = jnp.transpose(features[:, x].astype(F32), (1, 0, 2))
         cells_first[1 + x, pl.ds(1, 8)] = turned.astype(BF16)
     pack_edges(cells_first, pick, edge_first)
 
     pl.semaphore_wait(barrier, slab - 1 + 18)
-
-    for dy, dz in others:
-        pltpu.make_async_remote_copy(
-            src_ref=part_ref.at[at_y[dy] * n_gz + at_z[dz]],
-            dst_ref=sums_ref.at[mine],
-            send_sem=part_sem.at[0],
-            recv_sem=part_sem.at[1],
-            device_id=(me[0], at_y[dy], at_z[dz]),
-            device_id_type=MESH,
-        ).start()
 
     def start_halo(layer, cells_ref, edge_ref, got_ref):
         for n, move in enumerate(SIDES):
@@ -277,15 +265,32 @@
         for sem in range(2):
             wait_for(four, halo_sem.at[layer, sem])
 
-    def wait_across(layer, cells_ref, got_ref):
+    def wait_across(layer, cells_ref):
         twenty = cells_ref.at[pl.ds(0, 2), pl.ds(0, 10)]
         for sem in range(2):
             wait_for(twenty, halo_sem.at[layer, 2 + sem])
+
+    def wait_edges(layer, got_ref):
+        for sem in range(2):
             wait_for(got_ref, edge_sem.at[layer, sem])
 
     start_halo(0, cells_first, edge_first, got_first)
-
-    for fetch in fetches[5:]:
+    for fetch in fetches[1:4]:
+        fetch.wait()
+    paint(dest[...], cells[...], mass[...], live_ref[0], left_ref, right_ref, part_ref)
+    sums_ref[pl.ds(mine, 1)] = part_ref[pl.ds(mine, 1)]
+    for dy, dz in others:
+        pltpu.make_async_remote_copy(
+            src_ref=part_ref.at[at_y[dy] * n_gz + at_z[dz]],
+            dst_ref=sums_ref.at[mine],
+            send_sem=part_sem.at[0],
+            recv_sem=part_sem.at[1],
+            device_id=(me[0], at_y[dy], at_z[dz]),
+            device_id_type=MESH,
+        ).start()
+
+
+    for fetch in fetches[4:]:
         fetch.wait()
     style = style[...]
     modulate(layers[1], style, layers[0][...], main_first, ends_first)
@@ -296,52 +301,57 @@
 
     wait_beside(0, cells_first)
     convolve_own(cells_first, main_first, parts_ref)
+    wait_edges(0, got_first)
+    unpack_edges(got_first, ring_ref)
+    ends = convolve_ends(ring_ref, ends_first)
     rest = sums_ref.at[pl.ds(0, slab - 1)]
     wait_for(rest, part_sem.at[1])
     wait_for(rest, part_sem.at[0])
     density = sums_ref[0].astype(F32)
     for n in range(1, slab):
         density = density + sums_ref[n].astype(F32)
-    wait_across(0, cells_first, got_first)
-    unpack_edges(got_first, ring_ref)
+    wait_across(0, cells_first)
 
     def keep(row, values):
         cells_second[1 + row // 8, 1 + row % 8] = activate(
             values + gain_first * density[row : row + 1] + bias_first
         ).astype(BF16)
 
-    convolve_halo(cells_first, ring_ref, main_first, ends_first, parts_ref, keep)
+    convolve_halo(cells_first, ends, main_first, parts_ref, keep)
     pack_edges(cells_second, pick, edge_second)
     start_halo(1, cells_second, edge_second, got_second)
     wait_beside(1, cells_second)
     convolve_own(cells_second, main_second, parts_ref)
-    wait_across(1, cells_second, got_second)
+    wait_edges(1, got_second)
     unpack_edges(got_second, ring_ref)
+    ends_now = convolve_ends(ring_ref, ends_second)
+    wait_across(1, cells_second)
 
     def finish(row, values):
         out_ref[row // 8, row % 8] = activate(
             values + gain_second * density[row : row + 1] + bias_second
         ).astype(BF16)
 
-    convolve_halo(cells_second, ring_ref, main_second, ends_second, parts_ref, finish)
+    convolve_halo(cells_second, ends_now, main_second, parts_ref, finish)
 
 
 def shards(sizes, features, dest, cells, masses, live, style, *layers):
     slab = sizes[1] * sizes[2]
     operands = [
+        features,
         dest.reshape(1, -1),
         cells,
         masses,
-        live,
-        features,
         style.reshape(1, -1),
     ]
     for affine, kernel, bias, gain in (layers[:4], layers[4:]):
         operands += [affine.T, kernel, bias.reshape(1, -1), gain.reshape(1, -1)]
+    operands = [pltpu.with_memory_space_constraint(x, pltpu.HBM) for x in operands]
     result = pl.pallas_call(
         functools.partial(body, sizes, len(operands)),
-        out_shape=jax.ShapeDtypeStruct((2, 8, 64, 128), BF16),
-        in_specs=[pl.BlockSpec(memory_space=pltpu.HBM)] * len(operands),
+        out_shape=pltpu.VMEM((2, 8, 64, 128), BF16),
+        in_specs=[pl.BlockSpec(memory_space=pltpu.SMEM)]
+        + [pl.BlockSpec(memory_space=pltpu.HBM)] * len(operands),
         out_specs=pl.BlockSpec(memory_space=pltpu.VMEM),
         scratch_shapes=[pltpu.VMEM(x.shape, x.dtype) for x in operands]
         + [
@@ -367,10 +377,10 @@
             pltpu.SemaphoreType.DMA((2, 2)),
         ],
         compiler_params=pltpu.CompilerParams(
-            collective_id=0, has_side_effects=True, vmem_limit_bytes=63 * 1024 * 1024
+            collective_id=0, has_side_effects=True, vmem_limit_bytes=40 * 1024 * 1024
         ),
         name="styled_block",
-    )(*operands)
+    )(live, *operands)
     return result.transpose(2, 0, 1, 3)
 
 

time: 29.9 us -> 27.8 us (0.930)
  Pallas kernels: 27.3 us -> 26.2 us
  local copies, waits for them, and re-layouts: 1.83 us -> 0.88 us
    pallas_call x1, Pallas kernels: 27.3 us -> 26.2 us  [shards(): pl.pallas_call(functools.partial(body, sizes, len(operands)), out_shape=p...]
    transpose x1, local copies, waits for them, and re-layouts: 1.83 us -> 0.88 us  [shards(): return result.transpose(2, 0, 1, 3)]
where the time goes in v3:
time: 27.8 us; the launch traced here: 27.7 us
  Pallas kernels  26.2 us (94%)
  local copies, waits for them, and re-layouts  0.88 us (3%)
  between operations  0.66 us (2%)
    pallas_call x1, Pallas kernels, shards(): pl.pallas_call(functools.partial(body, sizes, len(operands)), out_shape=p...  26.2 us
    transpose x1, local copies, waits for them, and re-layouts, shards(): return result.transpose(2, 0, 1, 3)  0.88 us

profile of v3, /device:TPU:1, one launch (start us, length us, event | category | flops | bytes accessed | tf_op | source)
XLA Modules:
  0.0 27.7 jit_solution(2649132575322717296)
XLA Ops:
  0.7 26.2 %styled_block.1 = bf16[2,8,64,128]{3,2,1,0:T(8,128)(2,1)S(1)} custom-call(s32[1]{0:T(128)S(6)} %copy.16.live_ref, bf16[64,2,8,128]{3,2,1,0:T(8,128)(2,1)} %refs_0_.1, s32[1,32]{1,0:T(1,128)} %bitcast.13, s32[32,64]{1,0:T(8,128)} %refs_2_.1, bf16[32,64]{1,0:T(8,128)(2,1)} %refs_3_.1, f32[1,512]{1,0:T(1,128)} %bitcast.12, f32[64,512]{1,0:T(8,128)} %bitcast.10, ...), custom_call_target="tpu_custom_call" | custom-call | tf_op jit(solution)/shard_map/styled_block/pallas_call | solution.py:350
  26.8 0.9 %copy.15 = bf16[64,2,8,128]{3,2,1,0:T(8,128)(2,1)} copy(bf16[64,2,8,128]{3,0,2,1:T(8,128)(2,1)S(1)} %bitcast.9) | data formatting | bytes 524288 | tf_op jit(solution)/shard_map/transpose | solution.py:384

commit v4 on v3

--- a/solution.py
+++ b/solution.py
@@ -78,14 +78,13 @@
                     ring_ref[to_x, pl.ds(9, 1)] = tile[8 * x : 8 * x + 1]
 
 
-def stack(cells_ref, plane, y):
-    zero = jnp.zeros((64, 256), BF16)
+def stack(cells_ref, plane, y, last):
     return jnp.concatenate(
         [
             jnp.concatenate([cells_ref[plane, y + f], cells_ref[plane, y + f + 1]], axis=1)
             for f in range(3)
         ]
-        + [zero],
+        + [last],
         axis=0,
     )
 
@@ -95,14 +94,15 @@
 
 
 def convolve_own(cells_ref, main_ref, parts_ref):
+    zero = jnp.zeros((64, 256), BF16)
     for pair in range(4):
-        near = stack(cells_ref, 1, 2 * pair)
-        far = stack(cells_ref, 2, 2 * pair)
+        near = stack(cells_ref, 1, 2 * pair, zero)
+        far = stack(cells_ref, 2, 2 * pair, zero)
         parts_ref[pair] = taps(main_ref, 1, near) + taps(main_ref, 2, far)
         parts_ref[4 + pair] = taps(main_ref, 0, near) + taps(main_ref, 1, far)
 
 
-def convolve_ends(ring_ref, edge_ref):
+def convolve_ends(ring_ref, edge_ref, main_ref):
     window = jnp.concatenate(
         [
             jnp.concatenate([ring_ref[e + x, pl.ds(f, 8)] for x in range(2)], axis=0)
@@ -111,22 +111,31 @@
         ],
         axis=1,
     ).astype(BF16)
-    return lax.dot_general(edge_ref[...], window, NT, preferred_element_type=F32)
-
-
-def convolve_halo(cells_ref, ends, main_ref, parts_ref, emit):
+    ends = lax.dot_general(edge_ref[...], window, NT, preferred_element_type=F32)
+    high = ends.astype(BF16).astype(F32)
+    rest = ends - high
+    four = jnp.concatenate([high[:64], high[64:], rest[:64], rest[64:]], axis=1)
+    wide = jnp.concatenate([jnp.zeros((64, 64), F32), four], axis=1)
+    lane = lax.broadcasted_iota(jnp.int32, (64, 128), 1)
+    for e in (0, 2):
+        spot = pl.ds(256 * e + 128, 128)
+        kept = main_ref[pl.ds(64, 64), spot].astype(F32)
+        main_ref[pl.ds(64, 64), spot] = jnp.where(lane < 64, kept, wide).astype(BF16)
+
+
+def convolve_halo(cells_ref, main_ref, parts_ref, place_ref, emit):
     lane = lax.broadcasted_iota(jnp.int32, (64, 128), 1)
     for pair in range(8):
         x, y = pair // 4, 2 * (pair % 4)
-        parts = parts_ref[pair] + taps(main_ref, 2 * x, stack(cells_ref, 3 * x, y))
+        parts = parts_ref[pair] + taps(main_ref, 2 * x, stack(cells_ref, 3 * x, y, place_ref[pair]))
         for half in range(2):
             row = 8 * x + y + half
             lanes = slice(128 * half, 128 * half + 128)
             low = jnp.where(
-                lane == 0, ends[0:64, row : row + 1], pltpu.roll(parts[0:64, lanes], 1, 1)
+                lane == 0, 0.0, pltpu.roll(parts[0:64, lanes], 1, 1)
             )
             high = jnp.where(
-                lane == 127, ends[64:128, row : row + 1], pltpu.roll(parts[128:192, lanes], 127, 1)
+                lane == 127, 0.0, pltpu.roll(parts[128:192, lanes], 127, 1)
             )
             emit(row, low + parts[64:128, lanes] + high)
 
@@ -180,6 +189,7 @@
         ends_first,
         ends_second,
         parts_ref,
+        place_ref,
         fetch_sem,
         part_sem,
         halo_sem,
@@ -205,16 +215,16 @@
     for fetch in fetches[:4]:
         fetch.start()
     barrier = pltpu.get_barrier_semaphore()
-    for dy, dz in others:
-        pl.semaphore_signal(
-            barrier, inc=1, device_id=(me[0], at_y[dy], at_z[dz]), device_id_type=MESH
-        )
     for da in (-1, 1):
         for db in (-1, 0, 1):
             for dc in (-1, 0, 1):
                 pl.semaphore_signal(
                     barrier, inc=1, device_id=place((da, db, dc)), device_id_type=MESH
                 )
+    for dy, dz in others:
+        pl.semaphore_signal(
+            barrier, inc=1, device_id=(me[0], at_y[dy], at_z[dz]), device_id_type=MESH
+        )
     for fetch in fetches[4:]:
         fetch.start()
 
@@ -262,17 +272,19 @@
 
     def wait_beside(layer, cells_ref):
         four = cells_ref.at[pl.ds(0, 1), pl.ds(0, 4)]
-        for sem in range(2):
-            wait_for(four, halo_sem.at[layer, sem])
+        wait_for(four, halo_sem.at[layer, 1])
 
     def wait_across(layer, cells_ref):
         twenty = cells_ref.at[pl.ds(0, 2), pl.ds(0, 10)]
-        for sem in range(2):
-            wait_for(twenty, halo_sem.at[layer, 2 + sem])
+        wait_for(twenty, halo_sem.at[layer, 3])
 
     def wait_edges(layer, got_ref):
-        for sem in range(2):
-            wait_for(got_ref, edge_sem.at[layer, sem])
+        wait_for(got_ref, edge_sem.at[layer, 1])
+
+    def wait_sent(layer, cells_ref, got_ref):
+        wait_for(cells_ref.at[pl.ds(0, 1), pl.ds(0, 4)], halo_sem.at[layer, 0])
+        wait_for(cells_ref.at[pl.ds(0, 2), pl.ds(0, 10)], halo_sem.at[layer, 2])
+        wait_for(got_ref, edge_sem.at[layer, 0])
 
     start_halo(0, cells_first, edge_first, got_first)
     for fetch in fetches[1:4]:
@@ -290,6 +302,12 @@
         ).start()
 
 
+    nth = lax.broadcasted_iota(jnp.int32, (64, 256), 0) % 32
+    lane = lax.broadcasted_iota(jnp.int32, (64, 256), 1)
+    for pair in range(8):
+        target = 128 * (nth % 2) + 127 * (nth // 16)
+        hit = (nth % 16 // 2 == pair) & (lane == target)
+        place_ref[pair] = jnp.where(hit, 1.0, 0.0).astype(BF16)
     for fetch in fetches[4:]:
         fetch.wait()
     style = style[...]
@@ -303,10 +321,9 @@
     convolve_own(cells_first, main_first, parts_ref)
     wait_edges(0, got_first)
     unpack_edges(got_first, ring_ref)
-    ends = convolve_ends(ring_ref, ends_first)
+    convolve_ends(ring_ref, ends_first, main_first)
     rest = sums_ref.at[pl.ds(0, slab - 1)]
     wait_for(rest, part_sem.at[1])
-    wait_for(rest, part_sem.at[0])
     density = sums_ref[0].astype(F32)
     for n in range(1, slab):
         density = density + sums_ref[n].astype(F32)
@@ -317,14 +334,14 @@
             values + gain_first * density[row : row + 1] + bias_first
         ).astype(BF16)
 
-    convolve_halo(cells_first, ends, main_first, parts_ref, keep)
+    convolve_halo(cells_first, main_first, parts_ref, place_ref, keep)
     pack_edges(cells_second, pick, edge_second)
     start_halo(1, cells_second, edge_second, got_second)
     wait_beside(1, cells_second)
     convolve_own(cells_second, main_second, parts_ref)
     wait_edges(1, got_second)
     unpack_edges(got_second, ring_ref)
-    ends_now = convolve_ends(ring_ref, ends_second)
+    convolve_ends(ring_ref, ends_second, main_second)
     wait_across(1, cells_second)
 
     def finish(row, values):
@@ -332,7 +349,10 @@
             values + gain_second * density[row : row + 1] + bias_second
         ).astype(BF16)
 
-    convolve_halo(cells_second, ends_now, main_second, parts_ref, finish)
+    convolve_halo(cells_second, main_second, parts_ref, place_ref, finish)
+    wait_for(rest, part_sem.at[0])
+    wait_sent(0, cells_first, got_first)
+    wait_sent(1, cells_second, got_second)
 
 
 def shards(sizes, features, dest, cells, masses, live, style, *layers):
@@ -371,6 +391,7 @@
             pltpu.VMEM((128, 1152), BF16),
             pltpu.VMEM((128, 1152), BF16),
             pltpu.VMEM((8, 192, 256), F32),
+            pltpu.VMEM((8, 64, 256), BF16),
             pltpu.SemaphoreType.DMA((len(operands),)),
             pltpu.SemaphoreType.DMA((2,)),
             pltpu.SemaphoreType.DMA((2, 4)),

time: 27.8 us -> 27.5 us (0.989)
  Pallas kernels: 26.2 us -> 25.8 us
    pallas_call x1, Pallas kernels: 26.2 us -> 25.8 us  [shards(): pl.pallas_call(functools.partial(body, sizes, len(operands)), out_shape=p...]
where the time goes in v4:
time: 27.5 us; the launch traced here: 27.4 us
  Pallas kernels  25.8 us (94%)
  local copies, waits for them, and re-layouts  0.88 us (3%)
  between operations  0.66 us (2%)
    pallas_call x1, Pallas kernels, shards(): pl.pallas_call(functools.partial(body, sizes, len(operands)), out_shape=p...  25.8 us
    transpose x1, local copies, waits for them, and re-layouts, shards(): return result.transpose(2, 0, 1, 3)  0.88 us

profile of v4, /device:TPU:1, one launch (start us, length us, event | category | flops | bytes accessed | tf_op | source)
XLA Modules:
  0.0 27.4 jit_solution(18040707788674104120)
XLA Ops:
  0.7 25.8 %styled_block.1 = bf16[2,8,64,128]{3,2,1,0:T(8,128)(2,1)S(1)} custom-call(s32[1]{0:T(128)S(6)} %copy.16.live_ref, bf16[64,2,8,128]{3,2,1,0:T(8,128)(2,1)} %refs_0_.1, s32[1,32]{1,0:T(1,128)} %bitcast.13, s32[32,64]{1,0:T(8,128)} %refs_2_.1, bf16[32,64]{1,0:T(8,128)(2,1)} %refs_3_.1, f32[1,512]{1,0:T(1,128)} %bitcast.12, f32[64,512]{1,0:T(8,128)} %bitcast.10, ...), custom_call_target="tpu_custom_call" | custom-call | tf_op jit(solution)/shard_map/styled_block/pallas_call | solution.py:370
  26.5 0.9 %copy.15 = bf16[64,2,8,128]{3,2,1,0:T(8,128)(2,1)} copy(bf16[64,2,8,128]{3,0,2,1:T(8,128)(2,1)S(1)} %bitcast.9) | data formatting | bytes 524288 | tf_op jit(solution)/shard_map/transpose | solution.py:405

commit v5 on v4

--- a/solution.py
+++ b/solution.py
@@ -170,31 +170,27 @@
 
 def body(sizes, n_in, live_ref, *refs):
     sources = refs[:n_in]
-    out_ref = refs[n_in]
-    held = refs[n_in + 1 : 2 * n_in + 1]
+    cells_second, main_second, parts_ref, place_ref, addend_ref = refs[n_in : n_in + 5]
+    held = refs[n_in + 5 : 2 * n_in + 5]
     (
         left_ref,
         right_ref,
         part_ref,
         sums_ref,
         cells_first,
-        cells_second,
         edge_first,
         edge_second,
         got_first,
         got_second,
         ring_ref,
         main_first,
-        main_second,
         ends_first,
         ends_second,
-        parts_ref,
-        place_ref,
         fetch_sem,
         part_sem,
         halo_sem,
         edge_sem,
-    ) = refs[2 * n_in + 1 :]
+    ) = refs[2 * n_in + 5 :]
     n_gx, n_gy, n_gz = sizes
     slab = n_gy * n_gz
     me = (lax.axis_index("gx"), lax.axis_index("gy"), lax.axis_index("gz"))
@@ -337,6 +333,8 @@
     convolve_halo(cells_first, main_first, parts_ref, place_ref, keep)
     pack_edges(cells_second, pick, edge_second)
     start_halo(1, cells_second, edge_second, got_second)
+    for row in range(16):
+        addend_ref[row] = gain_second * density[row : row + 1] + bias_second
     wait_beside(1, cells_second)
     convolve_own(cells_second, main_second, parts_ref)
     wait_edges(1, got_second)
@@ -344,15 +342,26 @@
     convolve_ends(ring_ref, ends_second, main_second)
     wait_across(1, cells_second)
 
-    def finish(row, values):
-        out_ref[row // 8, row % 8] = activate(
-            values + gain_second * density[row : row + 1] + bias_second
-        ).astype(BF16)
-
-    convolve_halo(cells_second, main_second, parts_ref, place_ref, finish)
     wait_for(rest, part_sem.at[0])
     wait_sent(0, cells_first, got_first)
     wait_sent(1, cells_second, got_second)
+
+
+def last(cells_ref, main_ref, parts_ref, place_ref, addend_ref, out_ref, rows_ref, turned_ref, sems):
+    copies = [
+        pltpu.make_async_copy(turned_ref.at[x], out_ref.at[:, x], sems.at[x]) for x in range(2)
+    ]
+
+    def finish(row, values):
+        x = row // 8
+        rows_ref[x, row % 8] = activate(values + addend_ref[row])
+        if row % 8 == 7:
+            turned_ref[x] = jnp.transpose(rows_ref[x], (1, 0, 2)).astype(BF16)
+            copies[x].start()
+
+    convolve_halo(cells_ref, main_ref, parts_ref, place_ref, finish)
+    for copy in copies:
+        copy.wait()
 
 
 def shards(sizes, features, dest, cells, masses, live, style, *layers):
@@ -367,12 +376,19 @@
     for affine, kernel, bias, gain in (layers[:4], layers[4:]):
         operands += [affine.T, kernel, bias.reshape(1, -1), gain.reshape(1, -1)]
     operands = [pltpu.with_memory_space_constraint(x, pltpu.HBM) for x in operands]
+    vmem = pl.BlockSpec(memory_space=pltpu.VMEM)
     result = pl.pallas_call(
         functools.partial(body, sizes, len(operands)),
-        out_shape=pltpu.VMEM((2, 8, 64, 128), BF16),
+        out_shape=(
+            pltpu.VMEM((4, 10, 64, 128), BF16),
+            pltpu.VMEM((192, 768), BF16),
+            pltpu.VMEM((8, 192, 256), F32),
+            pltpu.VMEM((8, 64, 256), BF16),
+            pltpu.VMEM((16, 64, 128), F32),
+        ),
         in_specs=[pl.BlockSpec(memory_space=pltpu.SMEM)]
         + [pl.BlockSpec(memory_space=pltpu.HBM)] * len(operands),
-        out_specs=pl.BlockSpec(memory_space=pltpu.VMEM),
+        out_specs=(pl.BlockSpec(memory_space=pltpu.VMEM),) * 5,
         scratch_shapes=[pltpu.VMEM(x.shape, x.dtype) for x in operands]
         + [
             pltpu.VMEM((512, 2048), BF16),
@@ -380,18 +396,14 @@
             pltpu.VMEM((slab, 16, 128), BF16),
             pltpu.VMEM((slab, 16, 128), BF16),
             pltpu.VMEM((4, 10, 64, 128), BF16),
-            pltpu.VMEM((4, 10, 64, 128), BF16),
             pltpu.VMEM((16, 128), BF16),
             pltpu.VMEM((16, 128), BF16),
             pltpu.VMEM((18, 16, 128), BF16),
             pltpu.VMEM((18, 16, 128), BF16),
             pltpu.VMEM((4, 16, 128), F32),
             pltpu.VMEM((192, 768), BF16),
-            pltpu.VMEM((192, 768), BF16),
             pltpu.VMEM((128, 1152), BF16),
             pltpu.VMEM((128, 1152), BF16),
-            pltpu.VMEM((8, 192, 256), F32),
-            pltpu.VMEM((8, 64, 256), BF16),
             pltpu.SemaphoreType.DMA((len(operands),)),
             pltpu.SemaphoreType.DMA((2,)),
             pltpu.SemaphoreType.DMA((2, 4)),
@@ -402,7 +414,18 @@
         ),
         name="styled_block",
     )(live, *operands)
-    return result.transpose(2, 0, 1, 3)
+    return pl.pallas_call(
+        last,
+        out_shape=jax.ShapeDtypeStruct((64, 2, 8, 128), BF16),
+        in_specs=[vmem] * 5,
+        out_specs=pl.BlockSpec(memory_space=pltpu.HBM),
+        scratch_shapes=[
+            pltpu.VMEM((2, 8, 64, 128), F32),
+            pltpu.VMEM((2, 64, 8, 128), BF16),
+            pltpu.SemaphoreType.DMA((2,)),
+        ],
+        name="last_rows",
+    )(*(pltpu.with_memory_space_constraint(x, pltpu.VMEM) for x in result))
 
 
 def solution(mesh):

time: 27.5 us -> 27.4 us (level)
  local copies, waits for them, and re-layouts: 0.88 us -> 0 us
  Pallas kernels: 25.8 us -> 26.6 us
    transpose x1 -> x0, local copies, waits for them, and re-layouts: 0.88 us -> none  [shards(): return result.transpose(2, 0, 1, 3)]
    pallas_call x1 -> x2, Pallas kernels: 25.8 us -> 26.6 us  [the longest x1 25.3 us: shards(): pl.pallas_call(functools.partial(body, sizes, len(operands)), out_shape=(...]
where the time goes in v5:
time: 27.4 us; the launch traced here: 27.3 us
  Pallas kernels  26.6 us (97%)
  between operations  0.66 us (2%)
    pallas_call x1, Pallas kernels, shards(): pl.pallas_call(functools.partial(body, sizes, len(operands)), out_shape=(...  25.3 us
    pallas_call x1, Pallas kernels, shards(): pl.pallas_call(last, out_shape=jax.ShapeDtypeStruct((64, 2, 8, 128), BF16...  1.26 us

profile of v5, /device:TPU:1, one launch (start us, length us, event | category | flops | bytes accessed | tf_op | source)
XLA Modules:
  0.0 27.3 jit_solution(2778673833909726279)
XLA Ops:
  0.7 25.3 %styled_block.1 = (bf16[4,10,64,128]{3,2,1,0:T(8,128)(2,1)S(1)}, bf16[192,768]{1,0:T(8,128)(2,1)S(1)}, f32[8,192,256]{2,1,0:T(8,128)S(1)}, bf16[8,64,256]{2,1,0:T(8,128)(2,1)S(1)}, f32[16,64,128]{2,1,0:T(8,128)S(1)}) custom-call(s32[1]{0:T(128)S(6)} %copy.15.live_ref, bf16[64,2,8,128]{3,2,1,0:T(8,128)(2,1)} %refs_0_.1, s32[1,32]{1,0:T(1,128)} %bitcast.11, ...), custom_call_target="tpu_custom_call" | custom-call | tf_op jit(solution)/shard_map/styled_block/pallas_call | solution.py:380
  26.0 1.3 %last_rows.1 = bf16[64,2,8,128]{3,2,1,0:T(8,128)(2,1)} custom-call(bf16[4,10,64,128]{3,2,1,0:T(8,128)(2,1)S(1)} %get-tuple-element.10.cells_ref, bf16[192,768]{1,0:T(8,128)(2,1)S(1)} %get-tuple-element.11.main_ref, f32[8,192,256]{2,1,0:T(8,128)S(1)} %get-tuple-element.12.parts_ref, bf16[8,64,256]{2,1,0:T(8,128)(2,1)S(1)} %get-tuple-element.13.place_ref, ...), custom_call_target="tpu_custom_call" | custom-call | tf_op jit(solution)/shard_map/last_rows/pallas_call | solution.py:417

commit v6 on v5

--- a/solution.py
+++ b/solution.py
@@ -12,7 +12,7 @@
 BF16 = jnp.bfloat16
 NT = (((1,), (1,)), ((), ()))
 SIDES = [(da, db, dc) for da in (-1, 1, 0) for db in (-1, 1, 0) for dc in (-1, 1)]
-PLANAR = [(1, 1), (1, -1), (-1, 1), (-1, -1), (0, 1), (0, -1), (1, 0), (-1, 0)]
+PLANAR = [(0, 1), (0, -1), (1, 1), (1, -1), (-1, 1), (-1, -1), (1, 0), (-1, 0)]
 
 
 def column(row):
@@ -323,11 +323,13 @@
     density = sums_ref[0].astype(F32)
     for n in range(1, slab):
         density = density + sums_ref[n].astype(F32)
+    for row in range(16):
+        addend_ref[row] = gain_first * density[row : row + 1] + bias_first
     wait_across(0, cells_first)
 
     def keep(row, values):
         cells_second[1 + row // 8, 1 + row % 8] = activate(
-            values + gain_first * density[row : row + 1] + bias_first
+            values + addend_ref[row]
         ).astype(BF16)
 
     convolve_halo(cells_first, main_first, parts_ref, place_ref, keep)

time: 27.4 us -> 27.4 us (level)
  no operation moved by 1% of the time
where the time goes in v6:
time: 27.4 us; the launch traced here: 27.3 us
  Pallas kernels  26.6 us (97%)
  between operations  0.66 us (2%)
    pallas_call x1, Pallas kernels, shards(): pl.pallas_call(functools.partial(body, sizes, len(operands)), out_shape=(...  25.4 us
    pallas_call x1, Pallas kernels, shards(): pl.pallas_call(last, out_shape=jax.ShapeDtypeStruct((64, 2, 8, 128), BF16...  1.26 us

profile of v6, /device:TPU:1, one launch (start us, length us, event | category | flops | bytes accessed | tf_op | source)
XLA Modules:
  0.0 27.3 jit_solution(1366108742411223321)
XLA Ops:
  0.7 25.4 %styled_block.1 = (bf16[4,10,64,128]{3,2,1,0:T(8,128)(2,1)S(1)}, bf16[192,768]{1,0:T(8,128)(2,1)S(1)}, f32[8,192,256]{2,1,0:T(8,128)S(1)}, bf16[8,64,256]{2,1,0:T(8,128)(2,1)S(1)}, f32[16,64,128]{2,1,0:T(8,128)S(1)}) custom-call(s32[1]{0:T(128)S(6)} %copy.15.live_ref, bf16[64,2,8,128]{3,2,1,0:T(8,128)(2,1)} %refs_0_.1, s32[1,32]{1,0:T(1,128)} %bitcast.11, ...), custom_call_target="tpu_custom_call" | custom-call | tf_op jit(solution)/shard_map/styled_block/pallas_call | solution.py:382
  26.0 1.3 %last_rows.1 = bf16[64,2,8,128]{3,2,1,0:T(8,128)(2,1)} custom-call(bf16[4,10,64,128]{3,2,1,0:T(8,128)(2,1)S(1)} %get-tuple-element.10.cells_ref, bf16[192,768]{1,0:T(8,128)(2,1)S(1)} %get-tuple-element.11.main_ref, f32[8,192,256]{2,1,0:T(8,128)S(1)} %get-tuple-element.12.parts_ref, bf16[8,64,256]{2,1,0:T(8,128)(2,1)S(1)} %get-tuple-element.13.place_ref, ...), custom_call_target="tpu_custom_call" | custom-call | tf_op jit(solution)/shard_map/last_rows/pallas_call | solution.py:419

commit v7 on v4

--- a/solution.py
+++ b/solution.py
@@ -190,6 +190,7 @@
         ends_second,
         parts_ref,
         place_ref,
+        final_ref,
         fetch_sem,
         part_sem,
         halo_sem,
@@ -345,9 +346,12 @@
     wait_across(1, cells_second)
 
     def finish(row, values):
-        out_ref[row // 8, row % 8] = activate(
+        final_ref[row // 8, row % 8] = activate(
             values + gain_second * density[row : row + 1] + bias_second
-        ).astype(BF16)
+        )
+        if row % 8 == 7:
+            turned = jnp.transpose(final_ref[row // 8], (1, 0, 2))
+            out_ref[:, row // 8] = turned.astype(BF16)
 
     convolve_halo(cells_second, main_second, parts_ref, place_ref, finish)
     wait_for(rest, part_sem.at[0])
@@ -369,7 +373,7 @@
     operands = [pltpu.with_memory_space_constraint(x, pltpu.HBM) for x in operands]
     result = pl.pallas_call(
         functools.partial(body, sizes, len(operands)),
-        out_shape=pltpu.VMEM((2, 8, 64, 128), BF16),
+        out_shape=pltpu.VMEM((64, 2, 8, 128), BF16),
         in_specs=[pl.BlockSpec(memory_space=pltpu.SMEM)]
         + [pl.BlockSpec(memory_space=pltpu.HBM)] * len(operands),
         out_specs=pl.BlockSpec(memory_space=pltpu.VMEM),
@@ -392,6 +396,7 @@
             pltpu.VMEM((128, 1152), BF16),
             pltpu.VMEM((8, 192, 256), F32),
             pltpu.VMEM((8, 64, 256), BF16),
+            pltpu.VMEM((2, 8, 64, 128), F32),
             pltpu.SemaphoreType.DMA((len(operands),)),
             pltpu.SemaphoreType.DMA((2,)),
             pltpu.SemaphoreType.DMA((2, 4)),
@@ -402,7 +407,7 @@
         ),
         name="styled_block",
     )(live, *operands)
-    return result.transpose(2, 0, 1, 3)
+    return result
 
 
 def solution(mesh):

time: 27.5 us -> 27.4 us (level)
    transpose x1 -> x0, local copies, waits for them, and re-layouts: 0.88 us -> none  [shards(): return result.transpose(2, 0, 1, 3)]
    unnamed x0 -> x1, local copies, waits for them, and re-layouts: none -> 0.71 us
where the time goes in v7:
time: 27.4 us; the launch traced here: 27.3 us
  Pallas kernels  25.9 us (95%)
  local copies, waits for them, and re-layouts  0.71 us (3%)
  between operations  0.66 us (2%)
    pallas_call x1, Pallas kernels, shards(): pl.pallas_call(functools.partial(body, sizes, len(operands)), out_shape=p...  25.9 us
    unnamed x1, local copies, waits for them, and re-layouts  0.71 us

profile of v7, /device:TPU:1, one launch (start us, length us, event | category | flops | bytes accessed | tf_op | source)
XLA Modules:
  0.0 27.3 jit_solution(18207249920624109758)
XLA Ops:
  0.7 25.9 %styled_block.1 = bf16[64,2,8,128]{3,2,1,0:T(8,128)(2,1)S(1)} custom-call(s32[1]{0:T(128)S(6)} %copy.17.live_ref, bf16[64,2,8,128]{3,2,1,0:T(8,128)(2,1)} %refs_0_.1, s32[1,32]{1,0:T(1,128)} %bitcast.11, s32[32,64]{1,0:T(8,128)} %refs_2_.1, bf16[32,64]{1,0:T(8,128)(2,1)} %refs_3_.1, f32[1,512]{1,0:T(1,128)} %bitcast.10, f32[64,512]{1,0:T(8,128)} %bitcast.8, ...), custom_call_target="tpu_custom_call" | custom-call | tf_op jit(solution)/shard_map/styled_block/pallas_call | solution.py:374
  26.6 0.7 %copy.16 = bf16[64,2,8,128]{3,2,1,0:T(8,128)(2,1)} copy(bf16[64,2,8,128]{3,2,1,0:T(8,128)(2,1)S(1)} %styled_block.1) | data formatting | bytes 524288
